TPU v7x, 512 devices: a whole 4x8x8 slice. The times are simulated.
512 devices in a mesh: group: 8 (over z_hi, core), rows: 64 (over z_lo, x, y).
Axes of the slice: x: 4, y: 8, z: 8 (z_hi: 4, z_lo: 2; z = z_hi * 2 + z_lo), core: 2. Of those that a mesh axis runs over, the one named last changes fastest.
Arguments:
- illum_tilts: int32 [8, 2], P('group'), may hold values from -430 to 430
- index_layers: float32 [1, 2048, 2048], P(None, 'rows', 'group'), may hold values from -0.02 to 0.02
- measured: float32 [8, 2, 2048, 2048], P('group', None, 'rows'), may hold values from -4 to 4
Outputs:
- residual: float32 [8, 2, 2048, 2048], P('group', None, 'rows')
All inputs are finite; a program needn't handle non-finite values.
Results may differ from a plain program's by a relative error of at most 0.0003.
Values sent between devices are 32-bit elements; how exact they have to be, the bound alone decides.
A program may use at most 64 MiB of HBM per device.

v0:
```python
import math

import jax
import jax.numpy as jnp
from jax import lax
from jax.sharding import PartitionSpec as P

N = 2048


THICKNESS = 4.0
HIGHEST = lax.Precision.HIGHEST


def signed_from_position(position, radix_low):
    natural_k = position // 128 + radix_low * (position % 128)
    return jnp.where(natural_k < N // 2, natural_k, natural_k - N)


def pupil_parts(freq_rows, freq_cols):
    radius = freq_rows * freq_rows + freq_cols * freq_cols
    inside = 100 * radius < 9 * N * N
    radius_norm = radius.astype(jnp.float32) / float((N // 2) ** 2)
    axial_root = jnp.sqrt(1.0 - jnp.minimum(radius_norm, 0.36))
    phase_angle = 2.0 * math.pi * THICKNESS * (axial_root - 1.0)
    inside_mask = inside.astype(jnp.float32)
    return (inside_mask * jnp.cos(phase_angle), inside_mask * jnp.sin(phase_angle))


def dft_table(extent, sign):
    steps = jnp.arange(extent, dtype=jnp.int32)
    product = jnp.mod(steps[:, None] * steps[None, :], extent)
    phase_angle = product.astype(jnp.float32) * (sign * 2.0 * math.pi / extent)
    return (jnp.cos(phase_angle), jnp.sin(phase_angle))


def twiddle_table(radix_low, sign):
    low_steps = jnp.arange(radix_low, dtype=jnp.int32)[:, None]
    high_steps = jnp.arange(128, dtype=jnp.int32)[None, :]
    product = jnp.mod(low_steps * high_steps, N)
    phase_angle = product.astype(jnp.float32) * (sign * 2.0 * math.pi / N)
    return (jnp.cos(phase_angle), jnp.sin(phase_angle))


def real_blocks(table):
    cosine, sine = table
    return jnp.stack([jnp.stack([cosine, -sine]), jnp.stack([sine, cosine])])


def twist(section, cosine, sine):
    real_part = cosine * section[0] - sine * section[1]
    imag_part = cosine * section[1] + sine * section[0]
    return jnp.stack([real_part, imag_part])


def rotate(values, width):
    signs = jnp.concatenate([-jnp.ones((width,), jnp.float32), jnp.ones((width,), jnp.float32)])
    return signs * jnp.roll(values, width, axis=-1)


def apply_along(table, values, form, width):
    cosine, sine = table
    first = jnp.einsum(form, cosine, values, precision=HIGHEST)
    second = jnp.einsum(form, sine, values, precision=HIGHEST)
    return first + rotate(second, width)


def per_device(illum_tilts, index_layers, measured):
    rows_count = lax.axis_size("rows")
    strip = N // rows_count
    radix_low = N // 128
    sub_count = max(1, strip // 128)
    group_low = radix_low // sub_count
    group_high = max(1, 128 // strip)
    tail = min(128, strip)
    fwd_low = dft_table(radix_low, -1.0)
    fwd_high = dft_table(128, -1.0)
    inv_low = dft_table(radix_low, 1.0)
    inv_high = dft_table(128, 1.0)
    twist_fwd = twiddle_table(radix_low, -1.0)
    twist_inv = twiddle_table(radix_low, 1.0)
    row_low_fwd = real_blocks(fwd_low)
    row_high_fwd = real_blocks(fwd_high).reshape(2, 2, group_high, tail, 128)
    row_low_inv = real_blocks(inv_low)
    row_high_inv = real_blocks(inv_high).reshape(2, 2, 128, group_high, tail)
    row_index = lax.axis_index("rows")
    row_start = row_index * strip
    freq_rows = signed_from_position(jnp.arange(N, dtype=jnp.int32), radix_low)
    freq_cols = signed_from_position(row_start + jnp.arange(strip, dtype=jnp.int32), radix_low)
    pupil_real, pupil_imag = pupil_parts(freq_rows[:, None], freq_cols[None, :])
    pupil_real = jnp.concatenate([pupil_real, pupil_real], axis=1)
    pupil_imag = jnp.concatenate([pupil_imag, pupil_imag], axis=1)

    def row_forward(values):
        shaped = values.reshape(2, strip, radix_low, 128)
        section = jnp.einsum("qpkn,prnm->qrkm", row_low_fwd, shaped, precision=HIGHEST)
        section = twist(section, twist_fwd[0], twist_fwd[1])
        section = section.reshape(2, strip, group_low, sub_count, 128)
        result = jnp.einsum("qphcn,prgsn->rghqsc", row_high_fwd, section, precision=HIGHEST)
        return result.reshape(strip, rows_count, 2 * strip)

    def column_work(values, width):
        shaped = values.reshape(radix_low, 128, 2 * width)
        section = apply_along(fwd_low, shaped, "kn,nmc->kmc", width)
        section = twist_fwd[0][:, :, None] * section + twist_fwd[1][:, :, None] * rotate(
            section, width
        )
        section = apply_along(fwd_high, section, "kn,anc->akc", width)
        section = section.reshape(N, 2 * width)
        section = pupil_real * section + pupil_imag * rotate(section, width)
        section = section.reshape(radix_low, 128, 2 * width)
        section = apply_along(inv_high, section, "nk,akc->anc", width)
        section = twist_inv[0][:, :, None] * section + twist_inv[1][:, :, None] * rotate(
            section, width
        )
        section = apply_along(inv_low, section, "mk,knc->mnc", width)
        return section.reshape(N, 2 * width) * (1.0 / N)

    def row_inverse(values):
        shaped = values.reshape(group_low, group_high, strip, 2, sub_count, tail)
        section = jnp.einsum("qpnhc,ghrpsc->qrgsn", row_high_inv, shaped, precision=HIGHEST)
        section = section.reshape(2, strip, radix_low, 128)
        section = twist(section, twist_inv[0], twist_inv[1])
        result = jnp.einsum("qpmk,prkn->qrmn", row_low_inv, section, precision=HIGHEST)
        return result.reshape(2, strip, N) * (1.0 / N)

    def one_layer(wave_field, screen_cos, screen_sin):
        screened = twist(wave_field, screen_cos, screen_sin)
        sent = row_forward(screened)
        columns = lax.all_to_all(sent, "rows", split_axis=1, concat_axis=0, tiled=True).reshape(
            N, 2 * strip
        )
        columns = column_work(columns, strip).reshape(rows_count, strip, 2 * strip)
        returned = lax.all_to_all(columns, "rows", split_axis=0, concat_axis=0, tiled=True)
        return row_inverse(returned)

    row_pos = row_start + jnp.arange(strip, dtype=jnp.int32)
    col_pos = jnp.arange(N, dtype=jnp.int32)
    waves = []
    residue = jnp.mod(
        illum_tilts[0, 0] * row_pos[:, None] + illum_tilts[0, 1] * col_pos[None, :], N
    )
    phase_angle = residue.astype(jnp.float32) * (2.0 * math.pi / N)
    waves.append(jnp.stack([jnp.cos(phase_angle), jnp.sin(phase_angle)]))
    contrast = lax.all_gather(index_layers[0], "group", axis=1, tiled=True)
    phase_angle = 2.0 * math.pi * THICKNESS * contrast
    screen_cos = jnp.cos(phase_angle)
    screen_sin = jnp.sin(phase_angle)
    waves = [one_layer(wave_field, screen_cos, screen_sin) for wave_field in waves]
    return jnp.stack(waves) - measured


def solution(mesh):
    return jax.shard_map(
        per_device,
        mesh=mesh,
        in_specs=(P("group", None), P(None, "rows", "group"), P("group", None, "rows", None)),
        out_specs=P("group", None, "rows", None),
        check_vma=False,
    )
```

profile of v0, /device:TPU:1, one launch (start us, length us, event | category | flops | bytes accessed | tf_op | source)
XLA Modules:
  0.0 103.9 jit_solution(16273402591762310754)
XLA Ops:
  0.0 0.1 multiply_sine_fusion.2
  0.1 0.1 fusion.144
  0.1 0.1 multiply_sine_fusion.3
  0.2 1.3 %fusion.196 = (s32[1,1]{1,0:T(1,128)}, s32[1,1]{1,0:T(1,128)}) fusion(s32[1,2]{1,0:T(1,128)} %param.3), kind=kLoop, calls=%fused_computation.274 | loop fusion | bytes 16 | tf_op jit(solution)/shard_map/slice | solution.py:141
  1.5 0.6 iota_multiply_fusion
  2.1 21.8 %all-gather = f32[1,32,2048]{2,1,0:T(8,128)S(1)} all-gather(f32[1,32,256]{2,1,0:T(8,128)} %param.4), channel_id=2, replica_groups=mesh['group'=8,'rows'=64] {'group'}, dimensions={2}, use_global_device_ids=true | all-gather | bytes 294912 | tf_op jit(solution)/shard_map/all_gather | solution.py:145
  23.9 0.6 fusion.149
  24.5 2.0 %fusion.47 = (f32[4,8,16,128]{3,1,2,0:T(8,128)S(1)}, f32[4,8,16,128]{3,1,2,0:T(8,128)S(1)}) fusion(f32[1,32,2048]{2,1,0:T(8,128)S(1)} %all-gather, s32[2048]{0:T(1024)S(1)} %iota_multiply_fusion, s32[32]{0:T(128)S(1)} %fusion.149), kind=kLoop, calls=%fused_computation.83 | loop fusion | flops 1376256 | bytes 794752
  26.7 0.3 fusion.97
  27.0 0.6 convolution_bitcast_fusion.6
  27.6 0.1 multiply_subtract_fusion.1
  27.7 1.8 %convolution_bitcast_fusion = f32[32,16,4,2,1,32]{5,1,2,3,0,4:T(8,128)S(1)} fusion(f32[1,32,16,128]{3,2,0,1:T(8,128)S(1)} %get-tuple-element.8, f32[1,32,16,128]{3,2,0,1:T(8,128)S(1)} %get-tuple-element.7, f32[1,1,4,32,128]{4,3,1,2,0:T(8,128)S(1)} %get-tuple-element.36, f32[1,1,4,32,128]{4,3,1,2,0:T(8,128)S(1)} %get-tuple-element.35, ...), kind=kOutput, calls=%fused_computation.2 | convolution fusion | flops 402980864 | bytes 1245184 | tf_op jit(solution)/shard_map/qphcn,prgsn->rghqsc/dot_general | solution.py:99
  29.5 1.6 %copy.57 = f32[32,16,4,2,1,32]{5,3,0,2,1,4:T(2,128)S(1)} copy(f32[32,16,4,2,1,32]{5,1,2,3,0,4:T(8,128)S(1)} %convolution_bitcast_fusion) | data formatting | bytes 1048576 | tf_op jit(solution)/shard_map/reshape | solution.py:100
  31.1 1.1 %reshape.621 = f32[32,64,64]{2,0,1:T(8,128)S(1)} reshape(f32[32,16,4,2,1,32]{5,3,0,2,1,4:T(2,128)S(1)} %copy.57) | data formatting | bytes 1048576 | tf_op jit(solution)/shard_map/reshape | solution.py:100
  32.3 1.4 %reshape.622 = f32[64,1,2048]{2,1,0:T(1,128)} reshape(f32[64,32,64]{2,1,0:T(8,128)S(1)} %bitcast.177) | data formatting | bytes 1048576
  33.7 11.5 %all-to-all-start = ((f32[64,1,2048]{2,1,0:T(1,128)}), f32[64,1,2048]{2,1,0:T(1,128)S(1)}, u32[]{:S(2)}, u32[]{:S(2)}) async-start(f32[64,1,2048]{2,1,0:T(1,128)} %reshape.622), calls=%async_computation | async-start | bytes 1048576 | tf_op jit(solution)/shard_map/all_to_all | solution.py:130
  45.3 0.1 multiply_sine_fusion.4
  45.4 1.1 %fusion.30 = (f32[16,128,32]{1,0,2:T(8,128)S(1)}, f32[16,128,32]{1,0,2:T(8,128)S(1)}) fusion(s32[32]{0:T(128)S(1)} %fusion.146, s32[16,128]{1,0:T(8,128)S(1)} %fusion.107), kind=kLoop, calls=%fused_computation.58 | loop fusion | flops 720896 | bytes 532608 | tf_op jit(solution)/shard_map/mul | solution.py:27
  46.5 16.3 %all-to-all-done = f32[64,1,2048]{2,1,0:T(1,128)S(1)} async-done(((f32[64,1,2048]{2,1,0:T(1,128)}), f32[64,1,2048]{2,1,0:T(1,128)S(1)}, u32[]{:S(2)}, u32[]{:S(2)}) %all-to-all-start) | async-done | bytes 524320 | tf_op jit(solution)/shard_map/all_to_all | solution.py:130
  62.9 0.5 broadcast.1067
  63.4 1.8 %reduce = f32[64,2048]{1,0:T(8,128)S(1)} reduce(f32[64,1,2048]{2,1,0:T(1,128)S(1)} %all-to-all-done, f32[]{:T(128)} %broadcast.1067), dimensions={1}, to_apply=%all_to_all.14.reduce_sub_computation | reduce | bytes 1048580 | tf_op jit(solution)/shard_map/all_to_all | solution.py:130
  65.2 0.4 reshape.623
  65.6 0.0 copy-start.1
  65.6 0.4 copy.34
  66.0 0.6 fusion.110
  66.7 0.0 copy-done.1
  66.7 0.6 convolution_add_fusion.1
  67.4 0.8 convolution_bitcast_fusion.4
  68.2 0.8 fusion.6
  69.1 0.2 copy.77
  69.4 0.2 fusion.10
  69.6 0.8 convolution_bitcast_fusion.2
  70.5 0.8 fusion.7
  71.4 0.6 fusion.108
  72.1 0.7 fusion.9
  72.7 0.4 copy.40
  73.1 1.5 %reshape.624 = f32[64,1,2048]{2,1,0:T(1,128)} reshape(f32[64,32,64]{2,1,0:T(8,128)S(1)} %bitcast.179) | data formatting | bytes 1048576
  74.6 5.6 %all-to-all-start.1 = ((f32[64,1,2048]{2,1,0:T(1,128)}), f32[64,1,2048]{2,1,0:T(1,128)S(1)}, u32[]{:S(2)}, u32[]{:S(2)}) async-start(f32[64,1,2048]{2,1,0:T(1,128)} %reshape.624), calls=%async_computation.1 | async-start | bytes 1048576 | tf_op jit(solution)/shard_map/all_to_all | solution.py:134
  80.1 0.1 fusion.145
  80.2 0.1 multiply_sine_fusion.1
  80.3 0.3 fusion.98
  80.6 15.6 %all-to-all-done.1 = f32[64,1,2048]{2,1,0:T(1,128)S(1)} async-done(((f32[64,1,2048]{2,1,0:T(1,128)}), f32[64,1,2048]{2,1,0:T(1,128)S(1)}, u32[]{:S(2)}, u32[]{:S(2)}) %all-to-all-start.1) | async-done | bytes 524320 | tf_op jit(solution)/shard_map/all_to_all | solution.py:134
  96.2 1.8 %reduce.1 = f32[64,2048]{1,0:T(8,128)S(1)} reduce(f32[64,1,2048]{2,1,0:T(1,128)S(1)} %all-to-all-done.1, f32[]{:T(128)} %broadcast.1067), dimensions={1}, to_apply=%all_to_all.17.reduce_sub_computation | reduce | bytes 1048580 | tf_op jit(solution)/shard_map/all_to_all | solution.py:134
  98.0 0.4 reshape.625
  98.4 1.2 %reshape.595 = f32[16,4,32,2,32]{4,3,2,1,0:T(2,128)S(1)} reshape(f32[64,32,64]{2,1,0:T(8,128)S(1)} %reshape.625) | data formatting | bytes 1048576 | tf_op jit(solution)/shard_map/reshape.3
  99.6 1.8 %fusion.2 = f32[2,32,16,1,128]{4,1,0,2,3:T(8,128)S(1)} fusion(f32[16,4,32,2,32,1]{4,3,2,1,0,5:T(2,128)S(1)} %bitcast.175, f32[1,1,128,4,32]{2,4,1,3,0:T(8,128)S(1)} %get-tuple-element.33, f32[1,1,128,4,32]{2,4,1,3,0:T(8,128)S(1)} %get-tuple-element.32, f32[1,1,128,4,32]{2,4,1,3,0:T(8,128)S(1)} %get-tuple-element.31), kind=kOutput, calls=%fused_computation.3 | convolution fusion | flops 402849792 | bytes 1245184 | tf_op jit(solution)/shard_map/qpnhc,ghrpsc->qrgsn/dot_general | solution.py:121
  101.4 0.0 copy-start
  101.4 0.1 multiply_subtract_fusion
  101.5 0.9 fusion.8
  102.5 0.3 mul.1049
  102.8 0.0 copy-done
  102.8 1.1 %copy_subtract_fusion = f32[1,2,32,2048]{3,2,1,0:T(8,128)} fusion(f32[1,2,32,2048]{3,2,1,0:T(8,128)S(1)} %copy-done, f32[1,2,32,2048]{3,1,2,0:T(2,128)S(1)} %mul.1049), kind=kLoop, calls=%fused_computation.40 | loop fusion | flops 131072 | bytes 1572864 | tf_op jit(solution)/shard_map/sub | solution.py:150
  (17 shorter events, 0.5 us)
Async XLA Ops:
  33.7 29.1 %all-to-all-start = ((f32[64,1,2048]{2,1,0:T(1,128)}), f32[64,1,2048]{2,1,0:T(1,128)S(1)}, u32[]{:S(2)}, u32[]{:S(2)}) async-start(f32[64,1,2048]{2,1,0:T(1,128)} %reshape.622), calls=%async_computation | async-start | bytes 1048576 | tf_op jit(solution)/shard_map/all_to_all | solution.py:130
  65.6 1.1 %copy-start.1 = (f32[64]{0:T(128)S(1)}, f32[64]{0:T(128)}, u32[]{:S(2)}) copy-start(f32[64]{0:T(128)} %constant.171.clone.1) | copy-start | bytes 772
  74.6 21.6 %all-to-all-start.1 = ((f32[64,1,2048]{2,1,0:T(1,128)}), f32[64,1,2048]{2,1,0:T(1,128)S(1)}, u32[]{:S(2)}, u32[]{:S(2)}) async-start(f32[64,1,2048]{2,1,0:T(1,128)} %reshape.624), calls=%async_computation.1 | async-start | bytes 1048576 | tf_op jit(solution)/shard_map/all_to_all | solution.py:134
  101.4 1.3 %copy-start = (f32[1,2,32,2048]{3,2,1,0:T(8,128)S(1)}, f32[1,2,32,2048]{3,2,1,0:T(8,128)}, u32[]{:S(2)}) copy-start(f32[1,2,32,2048]{3,2,1,0:T(8,128)} %param.5) | copy-start | bytes 1572868
where the time goes:
time: 106 us; the launch traced here: 104 us
  waiting for transfers between devices  31.9 us (30%)
  blocking collectives  21.8 us (21%)
  starting transfers between devices  17.1 us (16%)
  local copies, waits for them, and re-layouts  11.1 us (10%)
  matrix products  11 us (10%)
  other arithmetic  10.5 us (10%)
    all_gather x1, blocking collectives, per_device(): contrast = lax.all_gather(index_layers[0], 'group', axis=1, tiled=True)  21.8 us
    all_to_all x1, waiting for transfers between devices, one_layer(): lax.all_to_all(sent, 'rows', split_axis=1, concat_axis=0, tiled=True)  16.3 us
    all_to_all x1, waiting for transfers between devices, one_layer(): lax.all_to_all(columns, 'rows', split_axis=0, concat_axis=0, tiled=True)  15.6 us
    all_to_all x1, starting transfers between devices, one_layer(): lax.all_to_all(sent, 'rows', split_axis=1, concat_axis=0, tiled=True)  11.5 us
    all_to_all x1, starting transfers between devices, one_layer(): lax.all_to_all(columns, 'rows', split_axis=0, concat_axis=0, tiled=True)  5.56 us
    unnamed x14, local copies, waits for them, and re-layouts  4.13 us
    dot_general x4, matrix products, apply_along(): first = jnp.einsum(form, cosine, values, precision=HIGHEST)  2.98 us
    dot_general x4, matrix products, apply_along(): second = jnp.einsum(form, sine, values, precision=HIGHEST)  2.91 us
  transfers between devices with their start and end apart: 2, of which 2 were waited for; matrix products, arithmetic and copies ran while one was open for 2% of the time, Pallas kernels for 0%

commit v1 on v0

v1 whole, which is shorter than its diff:
```python
import math

import jax
import jax.numpy as jnp
import ml_dtypes
import numpy as np
from jax import lax
from jax.experimental import pallas as pl
from jax.experimental.pallas import tpu as pltpu
from jax.sharding import PartitionSpec as P

N = 2048
THICKNESS = 4.0
MESH = pl.DeviceIdType.MESH

GROUPS = 8
ROWS = 64
STRIP = N // ROWS
LOW = 16
HIGH = 128
BANDS = 80
SUB = 5
FOLD = 4
MSG = 2 * SUB
TILES = LOW // FOLD
SLOTS = BANDS // SUB


def split_const(table):
    high = table.astype(ml_dtypes.bfloat16)
    low = (table - high.astype(np.float64)).astype(ml_dtypes.bfloat16)
    return high, low


def real_form(cosine, sine, order="out_in"):
    return np.block([[cosine, -sine], [sine, cosine]])


def tables():
    two_pi = 2.0 * math.pi
    m = np.arange(BANDS) - BANDS // 2
    angle = two_pi * ((m[:, None] * np.arange(HIGH)[None, :]) % HIGH) / HIGH
    forward = real_form(np.cos(angle), -np.sin(angle)).reshape(2, SLOTS, SUB, 2 * HIGH)
    col_fwd = forward.transpose(1, 0, 2, 3).reshape(2 * BANDS, 2 * HIGH)
    inverse = real_form(np.cos(angle.T), np.sin(angle.T)).reshape(2 * HIGH, 2, SLOTS, SUB)
    col_inv = inverse.transpose(2, 1, 3, 0).reshape(2 * BANDS, 2 * HIGH)
    step = np.arange(ROWS)
    angle = two_pi * ((step[:, None] * step[None, :]) % ROWS) / ROWS
    row_fwd = real_form(np.cos(angle), -np.sin(angle))
    row_inv = real_form(np.cos(angle), np.sin(angle))
    step = np.arange(STRIP)
    angle = two_pi * ((step[:, None] * step[None, :]) % STRIP) / STRIP
    eye = np.eye(FOLD)
    cosine, sine = np.kron(eye, np.cos(angle)), np.kron(eye, np.sin(angle))
    in_fwd = real_form(cosine, -sine).T
    in_inv = real_form(cosine, sine).T
    angle = two_pi * (np.arange(LOW)[:, None] * np.arange(HIGH)[None, :]) / N
    col_twist = np.stack([np.cos(angle), np.sin(angle)]).astype(np.float32)
    angle = two_pi * (np.arange(ROWS)[:, None] * np.arange(STRIP)[None, :]) / N
    row_twist = np.stack([np.tile(np.cos(angle), FOLD), np.tile(np.sin(angle), FOLD)]).astype(
        np.float32
    )
    wide = np.stack(split_const(np.concatenate([col_fwd, col_inv, in_fwd, in_inv])))
    narrow = np.stack(split_const(np.concatenate([row_fwd, row_inv])))
    return wide, narrow, col_twist, row_twist


COL_FWD = (0, 2 * BANDS)
COL_INV = (2 * BANDS, 2 * BANDS)
IN_FWD = (4 * BANDS, 2 * HIGH)
IN_INV = (4 * BANDS + 2 * HIGH, 2 * HIGH)
ROW_FWD = (0, 2 * ROWS)
ROW_INV = (2 * ROWS, 2 * ROWS)


def sincos_cycles(cycles):
    cycles = cycles - jnp.round(cycles)
    quarter = cycles * (0.5 * math.pi)
    square = quarter * quarter
    sine = quarter * (
        1.0 + square * (-1.0 / 6 + square * (1.0 / 120 + square * (-1.0 / 5040 + square * (1.0 / 362880))))
    )
    cosine = 1.0 + square * (
        -0.5 + square * (1.0 / 24 + square * (-1.0 / 720 + square * (1.0 / 40320 - square * (1.0 / 3628800))))
    )
    sine, cosine = 2.0 * sine * cosine, 1.0 - 2.0 * sine * sine
    sine, cosine = 2.0 * sine * cosine, 1.0 - 2.0 * sine * sine
    return cosine, sine


def sincos_small(angle):
    square = angle * angle
    sine = angle * (1.0 + square * (-1.0 / 6 + square * (1.0 / 120 - square * (1.0 / 5040))))
    cosine = 1.0 + square * (-0.5 + square * (1.0 / 24 + square * (-1.0 / 720 + square * (1.0 / 40320))))
    return cosine, sine


def cmul(a, b):
    return (a[0] * b[0] - a[1] * b[1], a[0] * b[1] + a[1] * b[0])


def cadd(a, b):
    return (a[0] + b[0], a[1] + b[1])


def csub(a, b):
    return (a[0] - b[0], a[1] - b[1])


def dft4(a, sign):
    even, odd = cadd(a[0], a[2]), cadd(a[1], a[3])
    even_d, odd_d = csub(a[0], a[2]), csub(a[1], a[3])
    turned = (-odd_d[1], odd_d[0]) if sign > 0 else (odd_d[1], -odd_d[0])
    return [cadd(even, odd), cadd(even_d, turned), csub(even, odd), csub(even_d, turned)]


def dft16(v, sign):
    half = math.sqrt(0.5)
    firsts = [dft4([v[4 * n1 + n2] for n1 in range(4)], sign) for n2 in range(4)]
    out = [None] * 16
    for k1 in range(4):
        column = []
        for n2 in range(4):
            re, im = firsts[n2][k1]
            turn = n2 * k1
            if turn == 2:
                re, im = (
                    (half * (re - im), half * (re + im)) if sign > 0 else (half * (re + im), half * (im - re))
                )
            elif turn == 4:
                re, im = (-im, re) if sign > 0 else (im, -re)
            elif turn == 6:
                re, im = (
                    (-half * (re + im), half * (re - im)) if sign > 0 else (half * (im - re), -half * (re + im))
                )
            elif turn:
                angle = 2.0 * math.pi * turn / 16
                re, im = cmul((re, im), (math.cos(angle), sign * math.sin(angle)))
            column.append((re, im))
        for k2, value in enumerate(dft4(column, sign)):
            out[k1 + 4 * k2] = value
    return out


def split(value):
    high = value.astype(jnp.bfloat16)
    low = (value - high.astype(jnp.float32)).astype(jnp.bfloat16)
    return high, low


def dot3(a, b, dims):
    def one(x, y):
        return lax.dot_general(x, y, (dims, ((), ())), preferred_element_type=jnp.float32)

    return one(a[0], b[0]) + (one(a[0], b[1]) + one(a[1], b[0]))


def pupil_parts(freq_rows, freq_cols):
    radius = freq_rows * freq_rows + freq_cols * freq_cols
    inside = 100 * radius < 9 * N * N
    radius_norm = radius.astype(jnp.float32) * (1.0 / float((N // 2) ** 2))
    axial_root = jnp.sqrt(1.0 - jnp.minimum(radius_norm, 0.36))
    cosine, sine = sincos_cycles(THICKNESS * (axial_root - 1.0))
    scale = jnp.where(inside, 1.0 / float(N * N), 0.0)
    return scale * cosine, scale * sine


def kernel(
    tilts, index_ref, wide, narrow, col_twist, row_twist, out_ref,
    strip, incident, section, send_a, recv_a, send_b, recv_b, pupil,
    gather_send, gather_recv, a_send, a_recv, b_send, b_recv,
):
    group = lax.axis_index("group")
    me = lax.axis_index("rows")

    def table(ref, place):
        rows = pl.ds(place[0], place[1])
        return ref[0, rows, :], ref[1, rows, :]

    barrier = pltpu.get_barrier_semaphore()

    def greet_group(step, carry):
        peer = lax.rem(group + step, GROUPS)
        pl.semaphore_signal(barrier, inc=1, device_id={"group": peer}, device_id_type=MESH)
        return carry

    def greet_rows(step, carry):
        peer = lax.rem(me + step, ROWS)
        pl.semaphore_signal(barrier, inc=1, device_id={"rows": peer}, device_id_type=MESH)
        return carry

    lax.fori_loop(1, GROUPS, greet_group, 0)
    lax.fori_loop(1, ROWS, greet_rows, 0)
    pl.semaphore_wait(barrier, GROUPS - 1 + ROWS - 1)

    gathers = []
    for step in range(1, GROUPS):
        peer = lax.rem(group + step, GROUPS)
        copy = pltpu.make_async_remote_copy(
            src_ref=index_ref,
            dst_ref=strip.at[group],
            send_sem=gather_send.at[step],
            recv_sem=gather_recv.at[step],
            device_id={"group": peer},
            device_id_type=MESH,
        )
        copy.start()
        gathers.append(copy)
    strip[group] = index_ref[...]

    tilt_row, tilt_col = tilts[0, 0], tilts[0, 1]
    pos_row = me * STRIP + lax.broadcasted_iota(jnp.int32, (STRIP, HIGH), 0)
    pos_col = lax.broadcasted_iota(jnp.int32, (STRIP, HIGH), 1)
    base = tilt_row * pos_row + tilt_col * pos_col
    for y1 in range(LOW):
        residue = (base + tilt_col * (HIGH * y1)) & (N - 1)
        cosine, sine = sincos_cycles(residue.astype(jnp.float32) * (1.0 / N))
        incident[0, y1] = cosine
        incident[1, y1] = sine

    lane = lax.broadcasted_iota(jnp.int32, (ROWS, FOLD * STRIP), 1)
    natural = lax.broadcasted_iota(jnp.int32, (ROWS, FOLD * STRIP), 0) + ROWS * lax.rem(lane, STRIP)
    freq_rows = jnp.where(natural < N // 2, natural, natural - N)
    tile_me = me // SLOTS
    slot_me = lax.rem(me, SLOTS)
    freq_cols = tile_me * FOLD + lane // STRIP + LOW * (slot_me * SUB - BANDS // 2)
    for sub in range(SUB):
        real, imag = pupil_parts(freq_rows, freq_cols + LOW * sub)
        pupil[0, sub] = real
        pupil[1, sub] = imag

    for copy in gathers:
        copy.wait()

    for part in range(STRIP // 8):
        rows = pl.ds(8 * part, 8)
        values = []
        for y1 in range(LOW):
            lanes = pl.ds(HIGH * (y1 % 2), HIGH)
            contrast = strip[y1 // 2, rows, lanes]
            screen = sincos_small(contrast * (2.0 * math.pi * THICKNESS))
            values.append(cmul(screen, (incident[0, y1, rows, :], incident[1, y1, rows, :])))
        values = dft16(values, -1)
        for kap in range(LOW):
            twist = (col_twist[0, pl.ds(kap, 1), :], -col_twist[1, pl.ds(kap, 1), :])
            real, imag = cmul(values[kap], twist)
            place = pl.ds(kap * STRIP + 8 * part, 8)
            section[place, pl.ds(0, HIGH)] = real
            section[place, pl.ds(HIGH, HIGH)] = imag

    forward = table(wide, COL_FWD)
    for tile in range(TILES):
        data = split(section[pl.ds(tile * FOLD * STRIP, FOLD * STRIP), :])
        send_a[pl.ds(tile * 2 * BANDS, 2 * BANDS), :] = dot3(forward, data, ((1,), (1,)))

    def exchange(source, target, send_sem, recv_sem):
        def send_one(step, carry):
            peer = lax.rem(me + step, ROWS)
            pltpu.make_async_remote_copy(
                src_ref=source.at[pl.ds(peer * MSG, MSG), :],
                dst_ref=target.at[pl.ds(me * MSG, MSG), :],
                send_sem=send_sem,
                recv_sem=recv_sem,
                device_id={"rows": peer},
                device_id_type=MESH,
            ).start()
            return carry

        lax.fori_loop(1, ROWS, send_one, 0)
        target[pl.ds(me * MSG, MSG), :] = source[pl.ds(me * MSG, MSG), :]
        every = pl.ds(0, (ROWS - 1) * MSG)
        return pltpu.make_async_remote_copy(
            src_ref=source.at[every, :],
            dst_ref=target.at[every, :],
            send_sem=send_sem,
            recv_sem=recv_sem,
            device_id={"rows": lax.rem(me + 1, ROWS)},
            device_id_type=MESH,
        )

    first = exchange(send_a, recv_a, a_send, a_recv)
    first.wait_recv()

    parts = [
        jnp.concatenate(
            [recv_a[pl.ds(sub, ROWS, stride=MSG), :], recv_a[pl.ds(SUB + sub, ROWS, stride=MSG), :]], axis=0
        )
        for sub in range(SUB)
    ]
    lanes = FOLD * STRIP
    data = split(jnp.concatenate(parts, axis=1))
    data = dot3(table(narrow, ROW_FWD), data, ((1,), (0,)))
    twist_cos, twist_sin = row_twist[0], row_twist[1]
    parts = []
    for sub in range(SUB):
        real, imag = data[:ROWS, sub * lanes : (sub + 1) * lanes], data[ROWS:, sub * lanes : (sub + 1) * lanes]
        parts.append(jnp.concatenate(cmul((real, imag), (twist_cos, -twist_sin)), axis=1))
    data = dot3(split(jnp.concatenate(parts, axis=0)), table(wide, IN_FWD), ((1,), (0,)))
    parts = []
    for sub in range(SUB):
        rows = slice(sub * ROWS, (sub + 1) * ROWS)
        real, imag = data[rows, :lanes], data[rows, lanes:]
        parts.append(jnp.concatenate(cmul((real, imag), (pupil[0, sub], pupil[1, sub])), axis=1))
    data = dot3(split(jnp.concatenate(parts, axis=0)), table(wide, IN_INV), ((1,), (0,)))
    parts = []
    for sub in range(SUB):
        rows = slice(sub * ROWS, (sub + 1) * ROWS)
        real, imag = data[rows, :lanes], data[rows, lanes:]
        parts.append(jnp.concatenate(cmul((real, imag), (twist_cos, twist_sin)), axis=0))
    data = dot3(table(narrow, ROW_INV), split(jnp.concatenate(parts, axis=1)), ((1,), (0,)))
    for sub in range(SUB):
        columns = slice(sub * lanes, (sub + 1) * lanes)
        send_b[pl.ds(sub, ROWS, stride=MSG), :] = data[:ROWS, columns]
        send_b[pl.ds(SUB + sub, ROWS, stride=MSG), :] = data[ROWS:, columns]

    second = exchange(send_b, recv_b, b_send, b_recv)
    second.wait_recv()

    inverse = table(wide, COL_INV)
    for tile in range(TILES):
        data = split(recv_b[pl.ds(tile * 2 * BANDS, 2 * BANDS), :].T)
        section[pl.ds(tile * lanes, lanes), :] = dot3(data, inverse, ((1,), (0,)))
    for part in range(STRIP // 8):
        values = []
        for kap in range(LOW):
            place = pl.ds(kap * STRIP + 8 * part, 8)
            twist = (col_twist[0, pl.ds(kap, 1), :], col_twist[1, pl.ds(kap, 1), :])
            values.append(cmul((section[place, pl.ds(0, HIGH)], section[place, pl.ds(HIGH, HIGH)]), twist))
        values = dft16(values, 1)
        for y1 in range(LOW):
            for plane in range(2):
                out_ref[plane, pl.ds(8 * part, 8), pl.ds(HIGH * y1, HIGH)] = values[y1][plane]

    first.wait_send()
    second.wait_send()


def per_device(illum_tilts, index_layers, measured):
    wide, narrow, col_twist, row_twist = tables()
    vmem = pl.BlockSpec(memory_space=pltpu.VMEM)
    field = pl.pallas_call(
        kernel,
        out_shape=jax.ShapeDtypeStruct((2, STRIP, N), jnp.float32),
        in_specs=[pl.BlockSpec(memory_space=pltpu.SMEM)] + [vmem] * 5,
        out_specs=vmem,
        scratch_shapes=[
            pltpu.VMEM((GROUPS, STRIP, N // GROUPS), jnp.float32),
            pltpu.VMEM((2, LOW, STRIP, HIGH), jnp.float32),
            pltpu.VMEM((LOW * STRIP, 2 * HIGH), jnp.float32),
            pltpu.VMEM((ROWS * MSG, FOLD * STRIP), jnp.float32),
            pltpu.VMEM((ROWS * MSG, FOLD * STRIP), jnp.float32),
            pltpu.VMEM((ROWS * MSG, FOLD * STRIP), jnp.float32),
            pltpu.VMEM((ROWS * MSG, FOLD * STRIP), jnp.float32),
            pltpu.VMEM((2, SUB, ROWS, FOLD * STRIP), jnp.float32),
            pltpu.SemaphoreType.DMA((GROUPS,)),
            pltpu.SemaphoreType.DMA((GROUPS,)),
            pltpu.SemaphoreType.DMA,
            pltpu.SemaphoreType.DMA,
            pltpu.SemaphoreType.DMA,
            pltpu.SemaphoreType.DMA,
        ],
        compiler_params=pltpu.CompilerParams(
            collective_id=0, has_side_effects=True, vmem_limit_bytes=32 * 1024 * 1024
        ),
    )(
        illum_tilts,
        index_layers[0],
        jnp.asarray(wide),
        jnp.asarray(narrow),
        jnp.asarray(col_twist),
        jnp.asarray(row_twist),
    )
    return field[None] - measured


def solution(mesh):
    return jax.shard_map(
        per_device,
        mesh=mesh,
        in_specs=(P("group", None), P(None, "rows", "group"), P("group", None, "rows", None)),
        out_specs=P("group", None, "rows", None),
        check_vma=False,
    )
```

time: 106 us -> 54.9 us (0.52); the launches traced: 104 us -> 54.4 us
  Pallas kernels: 0 us -> 48.5 us
  waiting for transfers between devices: 31.9 us -> 0 us
  blocking collectives: 21.8 us -> 0 us
  starting transfers between devices: 17.1 us -> 0 us
  matrix products: 11 us -> 0 us
  other arithmetic: 10.5 us -> 0.85 us
  local copies, waits for them, and re-layouts: 11.1 us -> 5.03 us
    pallas_call x0 -> x1, Pallas kernels: none -> 48.5 us  [per_device(): pl.pallas_call(kernel, out_shape=jax.ShapeDtypeStruct((2, STRIP, N), jnp....]
    all_to_all x2 -> x0, waiting for transfers between devices: 31.9 us -> none  [the longest x1 16.3 us: one_layer(): lax.all_to_all(sent, 'rows', split_axis=1, concat_axis=0, tiled=True)]
    all_gather x1 -> x0, blocking collectives: 21.8 us -> none  [per_device(): contrast = lax.all_gather(index_layers[0], 'group', axis=1, tiled=True)]
    all_to_all x2 -> x0, starting transfers between devices: 17.1 us -> none  [the longest x1 11.5 us: one_layer(): lax.all_to_all(sent, 'rows', split_axis=1, concat_axis=0, tiled=True)]
    dot_general x12 -> x0, matrix products: 11 us -> none  [the longest x4 2.98 us: apply_along(): first = jnp.einsum(form, cosine, values, precision=HIGHEST)]
    all_to_all x2 -> x0, other arithmetic: 3.59 us -> none  [the longest x1 1.8 us: one_layer(): lax.all_to_all(columns, 'rows', split_axis=0, concat_axis=0, tiled=True)]
    reshape x2 -> x0, local copies, waits for them, and re-layouts: 2.75 us -> none  [row_forward(): return result.reshape(strip, rows_count, 2 * strip)]
    mul x6 -> x0, other arithmetic: 2.38 us -> none  [the longest x1 1.13 us: pupil_parts(): inside_mask * jnp.sin(phase_angle)]
  transfers between devices with their start and end apart: 2 -> 0, of which waited for: 2 -> 0; matrix products, arithmetic and copies ran while one was open for 2% -> 0% of each run, Pallas kernels for 0% -> 0%
where the time goes in v1:
time: 54.9 us; the launch traced here: 54.4 us
  Pallas kernels  48.5 us (88%)
  local copies, waits for them, and re-layouts  5.03 us (9%)
  other arithmetic  0.85 us (2%)
    pallas_call x1, Pallas kernels, per_device(): pl.pallas_call(kernel, out_shape=jax.ShapeDtypeStruct((2, STRIP, N), jnp....  48.5 us
    unnamed x14, local copies, waits for them, and re-layouts  5.03 us

profile of v1, /device:TPU:1, one launch (start us, length us, event | category | flops | bytes accessed | tf_op | source)
XLA Modules:
  0.0 54.4 jit_solution(10657454607433382664)
XLA Ops:
  0.0 0.0 copy-start.5
  0.0 0.7 %copy-done.5 = s32[1,2]{1,0:T(1,128)S(1)} copy-done((s32[1,2]{1,0:T(1,128)S(1)}, s32[1,2]{1,0:T(1,128)}, u32[]{:S(2)}) %copy-start.5) | copy-done | bytes 32
  0.7 0.0 copy-start
  0.7 1.2 %copy-done = bf16[2,832,256]{2,1,0:T(8,128)(2,1)S(1)} copy-done((bf16[2,832,256]{2,1,0:T(8,128)(2,1)S(1)}, bf16[2,832,256]{2,1,0:T(8,128)(2,1)}, u32[]{:S(2)}) %copy-start) | copy-done | bytes 851992
  1.8 0.0 copy-start.1
  1.8 0.9 %copy-done.1 = bf16[2,256,128]{2,1,0:T(8,128)(2,1)S(1)} copy-done((bf16[2,256,128]{2,1,0:T(8,128)(2,1)S(1)}, bf16[2,256,128]{2,1,0:T(8,128)(2,1)}, u32[]{:S(2)}) %copy-start.1) | copy-done | bytes 131096
  2.7 0.0 copy-start.2
  2.7 0.8 %copy-done.2 = f32[2,64,128]{2,1,0:T(8,128)S(1)} copy-done((f32[2,64,128]{2,1,0:T(8,128)S(1)}, f32[2,64,128]{2,1,0:T(8,128)}, u32[]{:S(2)}) %copy-start.2) | copy-done | bytes 65560
  3.6 0.0 copy-start.3
  3.6 0.8 %copy-done.3 = f32[1,32,256]{2,1,0:T(8,128)S(1)} copy-done((f32[1,32,256]{2,1,0:T(8,128)S(1)}, f32[1,32,256]{2,1,0:T(8,128)}, u32[]{:S(2)}) %copy-start.3) | copy-done | bytes 32792
  4.3 0.0 copy-start.4
  4.3 0.7 %copy-done.4 = f32[2,16,128]{2,1,0:T(8,128)S(1)} copy-done((f32[2,16,128]{2,1,0:T(8,128)S(1)}, f32[2,16,128]{2,1,0:T(8,128)}, u32[]{:S(2)}) %copy-start.4) | copy-done | bytes 16408
  5.0 0.0 copy-start.6
  5.0 48.5 %shard_map.73 = f32[2,32,2048]{2,1,0:T(8,128)S(1)} custom-call(s32[1,2]{1,0:T(1,128)S(1)} %copy-done.5, f32[32,256]{1,0:T(8,128)S(1)} %bitcast.3, bf16[2,832,256]{2,1,0:T(8,128)(2,1)S(1)} %copy-done, bf16[2,256,128]{2,1,0:T(8,128)(2,1)S(1)} %copy-done.1, f32[2,16,128]{2,1,0:T(8,128)S(1)} %copy-done.4, f32[2,64,128]{2,1,0:T(8,128)S(1)} %copy-done.2), custom_call_target="tpu_custom_call" | custom-call | tf_op jit(solution)/shard_map/pallas_call | solution.py:341
  53.5 0.0 copy-done.6
  53.5 0.9 %bitcast_subtract_fusion = f32[1,2,32,2048]{3,2,1,0:T(8,128)} fusion(f32[1,2,32,2048]{3,2,1,0:T(8,128)S(1)} %copy-done.6, f32[2,32,2048]{2,1,0:T(8,128)S(1)} %shard_map.73), kind=kLoop, calls=%fused_computation | loop fusion | flops 131072 | bytes 1572864 | tf_op jit(solution)/shard_map/sub | solution.py:373
Async XLA Ops:
  0.0 0.7 %copy-start.5 = (s32[1,2]{1,0:T(1,128)S(1)}, s32[1,2]{1,0:T(1,128)}, u32[]{:S(2)}) copy-start(s32[1,2]{1,0:T(1,128)} %tilts.1) | copy-start | bytes 28
  0.7 1.2 %copy-start = (bf16[2,832,256]{2,1,0:T(8,128)(2,1)S(1)}, bf16[2,832,256]{2,1,0:T(8,128)(2,1)}, u32[]{:S(2)}) copy-start(bf16[2,832,256]{2,1,0:T(8,128)(2,1)} %constant.8.clone.wide) | copy-start | bytes 2555908
  1.8 0.9 %copy-start.1 = (bf16[2,256,128]{2,1,0:T(8,128)(2,1)S(1)}, bf16[2,256,128]{2,1,0:T(8,128)(2,1)}, u32[]{:S(2)}) copy-start(bf16[2,256,128]{2,1,0:T(8,128)(2,1)} %constant.9.clone.narrow) | copy-start | bytes 393220
  2.7 0.8 %copy-start.2 = (f32[2,64,128]{2,1,0:T(8,128)S(1)}, f32[2,64,128]{2,1,0:T(8,128)}, u32[]{:S(2)}) copy-start(f32[2,64,128]{2,1,0:T(8,128)} %constant.11.clone.row_twist) | copy-start | bytes 196612
  3.6 0.8 %copy-start.3 = (f32[1,32,256]{2,1,0:T(8,128)S(1)}, f32[1,32,256]{2,1,0:T(8,128)}, u32[]{:S(2)}) copy-start(f32[1,32,256]{2,1,0:T(8,128)} %param.8) | copy-start | bytes 98308
  4.3 0.7 %copy-start.4 = (f32[2,16,128]{2,1,0:T(8,128)S(1)}, f32[2,16,128]{2,1,0:T(8,128)}, u32[]{:S(2)}) copy-start(f32[2,16,128]{2,1,0:T(8,128)} %constant.10.clone.col_twist) | copy-start | bytes 49156
  5.0 48.5 %copy-start.6 = (f32[1,2,32,2048]{3,2,1,0:T(8,128)S(1)}, f32[1,2,32,2048]{3,2,1,0:T(8,128)}, u32[]{:S(2)}) copy-start(f32[1,2,32,2048]{3,2,1,0:T(8,128)} %param.9) | copy-start | bytes 1572868

commit v2 on v1

--- a/solution.py
+++ b/solution.py
@@ -32,7 +32,7 @@
     return high, low
 
 
-def real_form(cosine, sine, order="out_in"):
+def real_form(cosine, sine):
     return np.block([[cosine, -sine], [sine, cosine]])
 
 
@@ -166,96 +166,144 @@
 
 
 def kernel(
-    tilts, index_ref, wide, narrow, col_twist, row_twist, out_ref,
+    tilts_hbm, index_ref, wide_hbm, narrow_hbm, col_hbm, row_hbm, out_ref,
     strip, incident, section, send_a, recv_a, send_b, recv_b, pupil,
-    gather_send, gather_recv, a_send, a_recv, b_send, b_recv,
+    tilts, wide, narrow, col_twist, row_twist,
+    gather_send, gather_recv, pass_send, pass_recv, plane_sem, pair_sem, a_send, a_recv, b_send, b_recv, load_sems,
 ):
     group = lax.axis_index("group")
     me = lax.axis_index("rows")
+    loads = [
+        pltpu.make_async_copy(source, target, load_sems.at[place])
+        for place, (source, target) in enumerate(
+            [
+                (tilts_hbm, tilts),
+                (index_ref, strip.at[group]),
+                (col_hbm, col_twist),
+                (wide_hbm, wide),
+                (narrow_hbm, narrow),
+                (row_hbm, row_twist),
+            ]
+        )
+    ]
+    for load in loads:
+        load.start()
 
     def table(ref, place):
         rows = pl.ds(place[0], place[1])
         return ref[0, rows, :], ref[1, rows, :]
 
-    barrier = pltpu.get_barrier_semaphore()
-
-    def greet_group(step, carry):
-        peer = lax.rem(group + step, GROUPS)
-        pl.semaphore_signal(barrier, inc=1, device_id={"group": peer}, device_id_type=MESH)
-        return carry
-
-    def greet_rows(step, carry):
-        peer = lax.rem(me + step, ROWS)
-        pl.semaphore_signal(barrier, inc=1, device_id={"rows": peer}, device_id_type=MESH)
-        return carry
-
-    lax.fori_loop(1, GROUPS, greet_group, 0)
-    lax.fori_loop(1, ROWS, greet_rows, 0)
-    pl.semaphore_wait(barrier, GROUPS - 1 + ROWS - 1)
-
-    gathers = []
-    for step in range(1, GROUPS):
-        peer = lax.rem(group + step, GROUPS)
-        copy = pltpu.make_async_remote_copy(
-            src_ref=index_ref,
-            dst_ref=strip.at[group],
-            send_sem=gather_send.at[step],
-            recv_sem=gather_recv.at[step],
+    side = lax.rem(group, 2)
+    partner = group + 1 - 2 * side
+    place_z, place_x, place_y = me // 32, lax.rem(me // 8, 4), lax.rem(me, 8)
+    peers_y = [me - place_y + lax.rem(place_y + step, 8) for step in range(1, 8)]
+    peers_x = [me + 8 * (lax.rem(place_x + step, 4) - place_x) for step in range(1, 4)]
+    peer_z = me + 32 * (1 - 2 * place_z)
+    peers_group = [lax.rem(group + 2 * step, GROUPS) for step in (2, 1, 3)]
+
+    def signal(sem, axis, peer):
+        pl.semaphore_signal(sem, inc=1, device_id={axis: peer}, device_id_type=MESH)
+
+    with jax.named_scope("greet"):
+        barrier = pltpu.get_barrier_semaphore()
+        for peer in peers_group + [partner]:
+            signal(barrier, "group", peer)
+        for peer in peers_y + peers_x + [peer_z]:
+            signal(barrier, "rows", peer)
+        pl.semaphore_wait(barrier, 15)
+
+    def piece(owner, sems, slot, peer):
+        return pltpu.make_async_remote_copy(
+            src_ref=strip.at[owner],
+            dst_ref=strip.at[owner],
+            send_sem=sems[0].at[slot],
+            recv_sem=sems[1].at[slot],
             device_id={"group": peer},
             device_id_type=MESH,
         )
-        copy.start()
-        gathers.append(copy)
-    strip[group] = index_ref[...]
-
-    tilt_row, tilt_col = tilts[0, 0], tilts[0, 1]
-    pos_row = me * STRIP + lax.broadcasted_iota(jnp.int32, (STRIP, HIGH), 0)
-    pos_col = lax.broadcasted_iota(jnp.int32, (STRIP, HIGH), 1)
-    base = tilt_row * pos_row + tilt_col * pos_col
-    for y1 in range(LOW):
-        residue = (base + tilt_col * (HIGH * y1)) & (N - 1)
-        cosine, sine = sincos_cycles(residue.astype(jnp.float32) * (1.0 / N))
-        incident[0, y1] = cosine
-        incident[1, y1] = sine
-
-    lane = lax.broadcasted_iota(jnp.int32, (ROWS, FOLD * STRIP), 1)
-    natural = lax.broadcasted_iota(jnp.int32, (ROWS, FOLD * STRIP), 0) + ROWS * lax.rem(lane, STRIP)
-    freq_rows = jnp.where(natural < N // 2, natural, natural - N)
-    tile_me = me // SLOTS
-    slot_me = lax.rem(me, SLOTS)
-    freq_cols = tile_me * FOLD + lane // STRIP + LOW * (slot_me * SUB - BANDS // 2)
-    for sub in range(SUB):
-        real, imag = pupil_parts(freq_rows, freq_cols + LOW * sub)
-        pupil[0, sub] = real
-        pupil[1, sub] = imag
-
-    for copy in gathers:
-        copy.wait()
-
-    for part in range(STRIP // 8):
-        rows = pl.ds(8 * part, 8)
-        values = []
+
+    gather_sems, pass_sems = (gather_send, gather_recv), (pass_send, pass_recv)
+    with jax.named_scope("gather_start"):
+        loads[1].wait()
+        gathers = [piece(group, gather_sems, slot, peer) for slot, peer in enumerate(peers_group)]
+        passes = [piece(group, pass_sems, 3, partner)]
+        for copy in gathers + passes:
+            copy.start()
+    with jax.named_scope("report"):
+        for peer in peers_x:
+            signal(plane_sem, "rows", peer)
+        pl.semaphore_wait(plane_sem, 3)
+        signal(pair_sem, "rows", peer_z)
+        pl.semaphore_wait(pair_sem, 1)
+
+    with jax.named_scope("incident_pupil"):
+        loads[0].wait()
+        tilt_row, tilt_col = tilts[0, 0], tilts[0, 1]
+        pos_row = me * STRIP + lax.broadcasted_iota(jnp.int32, (STRIP, HIGH), 0)
+        pos_col = lax.broadcasted_iota(jnp.int32, (STRIP, HIGH), 1)
+        base = tilt_row * pos_row + tilt_col * pos_col
         for y1 in range(LOW):
-            lanes = pl.ds(HIGH * (y1 % 2), HIGH)
-            contrast = strip[y1 // 2, rows, lanes]
-            screen = sincos_small(contrast * (2.0 * math.pi * THICKNESS))
-            values.append(cmul(screen, (incident[0, y1, rows, :], incident[1, y1, rows, :])))
-        values = dft16(values, -1)
-        for kap in range(LOW):
-            twist = (col_twist[0, pl.ds(kap, 1), :], -col_twist[1, pl.ds(kap, 1), :])
-            real, imag = cmul(values[kap], twist)
-            place = pl.ds(kap * STRIP + 8 * part, 8)
-            section[place, pl.ds(0, HIGH)] = real
-            section[place, pl.ds(HIGH, HIGH)] = imag
-
-    forward = table(wide, COL_FWD)
-    for tile in range(TILES):
-        data = split(section[pl.ds(tile * FOLD * STRIP, FOLD * STRIP), :])
-        send_a[pl.ds(tile * 2 * BANDS, 2 * BANDS), :] = dot3(forward, data, ((1,), (1,)))
+            residue = (base + tilt_col * (HIGH * y1)) & (N - 1)
+            cosine, sine = sincos_cycles(residue.astype(jnp.float32) * (1.0 / N))
+            incident[0, y1] = cosine
+            incident[1, y1] = sine
+
+        lane = lax.broadcasted_iota(jnp.int32, (ROWS, FOLD * STRIP), 1)
+        natural = lax.broadcasted_iota(jnp.int32, (ROWS, FOLD * STRIP), 0) + ROWS * lax.rem(lane, STRIP)
+        freq_rows = jnp.where(natural < N // 2, natural, natural - N)
+        tile_me = me // SLOTS
+        slot_me = lax.rem(me, SLOTS)
+        freq_cols = tile_me * FOLD + lane // STRIP + LOW * (slot_me * SUB - BANDS // 2)
+        for sub in range(SUB):
+            real, imag = pupil_parts(freq_rows, freq_cols + LOW * sub)
+            pupil[0, sub] = real
+            pupil[1, sub] = imag
+
+    with jax.named_scope("gather_wait"):
+        for slot, step in ((1, 3), (2, 1), (0, 2)):
+            gathers[slot].wait_recv()
+            copy = piece(lax.rem(group + 2 * step, GROUPS), pass_sems, slot, partner)
+            copy.start()
+            passes.append(copy)
+        for copy in passes:
+            copy.wait()
+        for copy in gathers:
+            copy.wait_send()
+        for place in (2, 3, 4, 5):
+            loads[place].wait()
+
+    with jax.named_scope("screen_dft16"):
+        for part in range(STRIP // 8):
+            rows = pl.ds(8 * part, 8)
+            values = []
+            for y1 in range(LOW):
+                lanes = pl.ds(HIGH * (y1 % 2), HIGH)
+                contrast = strip[y1 // 2, rows, lanes]
+                screen = sincos_small(contrast * (2.0 * math.pi * THICKNESS))
+                values.append(cmul(screen, (incident[0, y1, rows, :], incident[1, y1, rows, :])))
+            values = dft16(values, -1)
+            for kap in range(LOW):
+                twist = (col_twist[0, pl.ds(kap, 1), :], -col_twist[1, pl.ds(kap, 1), :])
+                real, imag = cmul(values[kap], twist)
+                place = pl.ds(kap * STRIP + 8 * part, 8)
+                section[place, pl.ds(0, HIGH)] = real
+                section[place, pl.ds(HIGH, HIGH)] = imag
+
+    with jax.named_scope("column_128"):
+        forward = table(wide, COL_FWD)
+        for tile in range(TILES):
+            data = split(section[pl.ds(tile * FOLD * STRIP, FOLD * STRIP), :])
+            send_a[pl.ds(tile * 2 * BANDS, 2 * BANDS), :] = dot3(forward, data, ((1,), (1,)))
 
     def exchange(source, target, send_sem, recv_sem):
+        def far_first(step, size):
+            return lax.rem(size // 2 + size + (1 - 2 * lax.rem(step, 2)) * ((step + 1) // 2), size)
+
         def send_one(step, carry):
-            peer = lax.rem(me + step, ROWS)
+            to_y = lax.rem(place_y + far_first(step // 8, 8), 8)
+            to_x = lax.rem(place_x + far_first(lax.rem(step // 2, 4), 4), 4)
+            to_z = lax.rem(place_z + 1 + lax.rem(step, 2), 2)
+            peer = to_z * 32 + to_x * 8 + to_y
             pltpu.make_async_remote_copy(
                 src_ref=source.at[pl.ds(peer * MSG, MSG), :],
                 dst_ref=target.at[pl.ds(me * MSG, MSG), :],
@@ -266,7 +314,7 @@
             ).start()
             return carry
 
-        lax.fori_loop(1, ROWS, send_one, 0)
+        lax.fori_loop(0, ROWS - 1, send_one, 0)
         target[pl.ds(me * MSG, MSG), :] = source[pl.ds(me * MSG, MSG), :]
         every = pl.ds(0, (ROWS - 1) * MSG)
         return pltpu.make_async_remote_copy(
@@ -278,58 +326,64 @@
             device_id_type=MESH,
         )
 
-    first = exchange(send_a, recv_a, a_send, a_recv)
-    first.wait_recv()
-
-    parts = [
-        jnp.concatenate(
-            [recv_a[pl.ds(sub, ROWS, stride=MSG), :], recv_a[pl.ds(SUB + sub, ROWS, stride=MSG), :]], axis=0
-        )
-        for sub in range(SUB)
-    ]
-    lanes = FOLD * STRIP
-    data = split(jnp.concatenate(parts, axis=1))
-    data = dot3(table(narrow, ROW_FWD), data, ((1,), (0,)))
-    twist_cos, twist_sin = row_twist[0], row_twist[1]
-    parts = []
-    for sub in range(SUB):
-        real, imag = data[:ROWS, sub * lanes : (sub + 1) * lanes], data[ROWS:, sub * lanes : (sub + 1) * lanes]
-        parts.append(jnp.concatenate(cmul((real, imag), (twist_cos, -twist_sin)), axis=1))
-    data = dot3(split(jnp.concatenate(parts, axis=0)), table(wide, IN_FWD), ((1,), (0,)))
-    parts = []
-    for sub in range(SUB):
-        rows = slice(sub * ROWS, (sub + 1) * ROWS)
-        real, imag = data[rows, :lanes], data[rows, lanes:]
-        parts.append(jnp.concatenate(cmul((real, imag), (pupil[0, sub], pupil[1, sub])), axis=1))
-    data = dot3(split(jnp.concatenate(parts, axis=0)), table(wide, IN_INV), ((1,), (0,)))
-    parts = []
-    for sub in range(SUB):
-        rows = slice(sub * ROWS, (sub + 1) * ROWS)
-        real, imag = data[rows, :lanes], data[rows, lanes:]
-        parts.append(jnp.concatenate(cmul((real, imag), (twist_cos, twist_sin)), axis=0))
-    data = dot3(table(narrow, ROW_INV), split(jnp.concatenate(parts, axis=1)), ((1,), (0,)))
-    for sub in range(SUB):
-        columns = slice(sub * lanes, (sub + 1) * lanes)
-        send_b[pl.ds(sub, ROWS, stride=MSG), :] = data[:ROWS, columns]
-        send_b[pl.ds(SUB + sub, ROWS, stride=MSG), :] = data[ROWS:, columns]
-
-    second = exchange(send_b, recv_b, b_send, b_recv)
-    second.wait_recv()
-
-    inverse = table(wide, COL_INV)
-    for tile in range(TILES):
-        data = split(recv_b[pl.ds(tile * 2 * BANDS, 2 * BANDS), :].T)
-        section[pl.ds(tile * lanes, lanes), :] = dot3(data, inverse, ((1,), (0,)))
-    for part in range(STRIP // 8):
-        values = []
-        for kap in range(LOW):
-            place = pl.ds(kap * STRIP + 8 * part, 8)
-            twist = (col_twist[0, pl.ds(kap, 1), :], col_twist[1, pl.ds(kap, 1), :])
-            values.append(cmul((section[place, pl.ds(0, HIGH)], section[place, pl.ds(HIGH, HIGH)]), twist))
-        values = dft16(values, 1)
-        for y1 in range(LOW):
-            for plane in range(2):
-                out_ref[plane, pl.ds(8 * part, 8), pl.ds(HIGH * y1, HIGH)] = values[y1][plane]
+    with jax.named_scope("exchange_a_start"):
+        first = exchange(send_a, recv_a, a_send, a_recv)
+    with jax.named_scope("exchange_a_wait"):
+        first.wait_recv()
+
+    with jax.named_scope("row_work"):
+        parts = [
+            jnp.concatenate(
+                [recv_a[pl.ds(sub, ROWS, stride=MSG), :], recv_a[pl.ds(SUB + sub, ROWS, stride=MSG), :]], axis=0
+            )
+            for sub in range(SUB)
+        ]
+        lanes = FOLD * STRIP
+        data = split(jnp.concatenate(parts, axis=1))
+        data = dot3(table(narrow, ROW_FWD), data, ((1,), (0,)))
+        twist_cos, twist_sin = row_twist[0], row_twist[1]
+        parts = []
+        for sub in range(SUB):
+            real, imag = data[:ROWS, sub * lanes : (sub + 1) * lanes], data[ROWS:, sub * lanes : (sub + 1) * lanes]
+            parts.append(jnp.concatenate(cmul((real, imag), (twist_cos, -twist_sin)), axis=1))
+        data = dot3(split(jnp.concatenate(parts, axis=0)), table(wide, IN_FWD), ((1,), (0,)))
+        parts = []
+        for sub in range(SUB):
+            rows = slice(sub * ROWS, (sub + 1) * ROWS)
+            real, imag = data[rows, :lanes], data[rows, lanes:]
+            parts.append(jnp.concatenate(cmul((real, imag), (pupil[0, sub], pupil[1, sub])), axis=1))
+        data = dot3(split(jnp.concatenate(parts, axis=0)), table(wide, IN_INV), ((1,), (0,)))
+        parts = []
+        for sub in range(SUB):
+            rows = slice(sub * ROWS, (sub + 1) * ROWS)
+            real, imag = data[rows, :lanes], data[rows, lanes:]
+            parts.append(jnp.concatenate(cmul((real, imag), (twist_cos, twist_sin)), axis=0))
+        data = dot3(table(narrow, ROW_INV), split(jnp.concatenate(parts, axis=1)), ((1,), (0,)))
+        for sub in range(SUB):
+            columns = slice(sub * lanes, (sub + 1) * lanes)
+            send_b[pl.ds(sub, ROWS, stride=MSG), :] = data[:ROWS, columns]
+            send_b[pl.ds(SUB + sub, ROWS, stride=MSG), :] = data[ROWS:, columns]
+
+    with jax.named_scope("exchange_b_start"):
+        second = exchange(send_b, recv_b, b_send, b_recv)
+    with jax.named_scope("exchange_b_wait"):
+        second.wait_recv()
+
+    with jax.named_scope("columns_back"):
+        inverse = table(wide, COL_INV)
+        for tile in range(TILES):
+            data = split(recv_b[pl.ds(tile * 2 * BANDS, 2 * BANDS), :].T)
+            section[pl.ds(tile * lanes, lanes), :] = dot3(data, inverse, ((1,), (0,)))
+        for part in range(STRIP // 8):
+            values = []
+            for kap in range(LOW):
+                place = pl.ds(kap * STRIP + 8 * part, 8)
+                twist = (col_twist[0, pl.ds(kap, 1), :], col_twist[1, pl.ds(kap, 1), :])
+                values.append(cmul((section[place, pl.ds(0, HIGH)], section[place, pl.ds(HIGH, HIGH)]), twist))
+            values = dft16(values, 1)
+            for y1 in range(LOW):
+                for plane in range(2):
+                    out_ref[plane, pl.ds(8 * part, 8), pl.ds(HIGH * y1, HIGH)] = values[y1][plane]
 
     first.wait_send()
     second.wait_send()
@@ -341,7 +395,7 @@
     field = pl.pallas_call(
         kernel,
         out_shape=jax.ShapeDtypeStruct((2, STRIP, N), jnp.float32),
-        in_specs=[pl.BlockSpec(memory_space=pltpu.SMEM)] + [vmem] * 5,
+        in_specs=[pl.BlockSpec(memory_space=pltpu.HBM)] * 6,
         out_specs=vmem,
         scratch_shapes=[
             pltpu.VMEM((GROUPS, STRIP, N // GROUPS), jnp.float32),
@@ -352,15 +406,25 @@
             pltpu.VMEM((ROWS * MSG, FOLD * STRIP), jnp.float32),
             pltpu.VMEM((ROWS * MSG, FOLD * STRIP), jnp.float32),
             pltpu.VMEM((2, SUB, ROWS, FOLD * STRIP), jnp.float32),
-            pltpu.SemaphoreType.DMA((GROUPS,)),
-            pltpu.SemaphoreType.DMA((GROUPS,)),
+            pltpu.SMEM((1, 2), jnp.int32),
+            pltpu.VMEM(wide.shape, jnp.bfloat16),
+            pltpu.VMEM(narrow.shape, jnp.bfloat16),
+            pltpu.VMEM(col_twist.shape, jnp.float32),
+            pltpu.VMEM(row_twist.shape, jnp.float32),
+            pltpu.SemaphoreType.DMA((3,)),
+            pltpu.SemaphoreType.DMA((3,)),
+            pltpu.SemaphoreType.DMA((4,)),
+            pltpu.SemaphoreType.DMA((4,)),
+            pltpu.SemaphoreType.REGULAR,
+            pltpu.SemaphoreType.REGULAR,
             pltpu.SemaphoreType.DMA,
             pltpu.SemaphoreType.DMA,
             pltpu.SemaphoreType.DMA,
             pltpu.SemaphoreType.DMA,
+            pltpu.SemaphoreType.DMA((6,)),
         ],
         compiler_params=pltpu.CompilerParams(
-            collective_id=0, has_side_effects=True, vmem_limit_bytes=32 * 1024 * 1024
+            collective_id=0, has_side_effects=True, vmem_limit_bytes=60 * 1024 * 1024
         ),
     )(
         illum_tilts,

time: 54.9 us -> 48.1 us (0.88)
  local copies, waits for them, and re-layouts: 5.03 us -> 0.01 us
  Pallas kernels: 48.5 us -> 46.1 us
  other arithmetic: 0.85 us -> 1.89 us
    unnamed x14 -> x2, local copies, waits for them, and re-layouts: 5.03 us -> 0.01 us
    pallas_call x1, Pallas kernels: 48.5 us -> 46.1 us  [per_device(): pl.pallas_call(kernel, out_shape=jax.ShapeDtypeStruct((2, STRIP, N), jnp....]
    sub x1, other arithmetic: 0.85 us -> 1.89 us  [per_device(): return field[None] - measured]
where the time goes in v2:
time: 48.1 us; the launch traced here: 48 us
  Pallas kernels  46.1 us (96%)
  other arithmetic  1.89 us (4%)
    pallas_call x1, Pallas kernels, per_device(): pl.pallas_call(kernel, out_shape=jax.ShapeDtypeStruct((2, STRIP, N), jnp....  46.1 us
    sub x1, other arithmetic, per_device(): return field[None] - measured  1.89 us

profile of v2, /device:TPU:1, one launch (start us, length us, event | category | flops | bytes accessed | tf_op | source)
XLA Modules:
  0.0 48.0 jit_solution(9450381731085871913)
XLA Ops:
  0.0 0.0 copy-start
  0.0 46.1 %shard_map.73 = f32[2,32,2048]{2,1,0:T(8,128)} custom-call(s32[1,2]{1,0:T(1,128)} %tilts_hbm.1, f32[32,256]{1,0:T(8,128)} %bitcast.3, bf16[2,832,256]{2,1,0:T(8,128)(2,1)} %constant.8.clone.wide_hbm, bf16[2,256,128]{2,1,0:T(8,128)(2,1)} %constant.9.clone.narrow_hbm, f32[2,16,128]{2,1,0:T(8,128)} %constant.10.clone.col_hbm, f32[2,64,128]{2,1,0:T(8,128)} %constant.11.clone.row_hbm), custom_call_target="tpu_custom_call" | custom-call | tf_op jit(solution)/shard_map/pallas_call | solution.py:395
  46.1 0.0 copy-done
  46.1 1.9 %bitcast_subtract_fusion = f32[1,2,32,2048]{3,2,1,0:T(8,128)} fusion(f32[1,2,32,2048]{3,2,1,0:T(8,128)S(1)} %copy-done, f32[2,32,2048]{2,1,0:T(8,128)} %shard_map.73), kind=kLoop, calls=%fused_computation | loop fusion | flops 131072 | bytes 1572864 | tf_op jit(solution)/shard_map/sub | solution.py:437
Async XLA Ops:
  0.0 46.1 %copy-start = (f32[1,2,32,2048]{3,2,1,0:T(8,128)S(1)}, f32[1,2,32,2048]{3,2,1,0:T(8,128)}, u32[]{:S(2)}) copy-start(f32[1,2,32,2048]{3,2,1,0:T(8,128)} %param.9) | copy-start | bytes 1572868

commit v3 on v2

--- a/solution.py
+++ b/solution.py
@@ -21,7 +21,7 @@
 BANDS = 80
 SUB = 5
 FOLD = 4
-MSG = 2 * SUB
+CHUNKS = ((0, 2), (2, 4), (4, 5))
 TILES = LOW // FOLD
 SLOTS = BANDS // SUB
 
@@ -41,9 +41,13 @@
     m = np.arange(BANDS) - BANDS // 2
     angle = two_pi * ((m[:, None] * np.arange(HIGH)[None, :]) % HIGH) / HIGH
     forward = real_form(np.cos(angle), -np.sin(angle)).reshape(2, SLOTS, SUB, 2 * HIGH)
-    col_fwd = forward.transpose(1, 0, 2, 3).reshape(2 * BANDS, 2 * HIGH)
+    forward = forward.transpose(1, 0, 2, 3)
     inverse = real_form(np.cos(angle.T), np.sin(angle.T)).reshape(2 * HIGH, 2, SLOTS, SUB)
-    col_inv = inverse.transpose(2, 1, 3, 0).reshape(2 * BANDS, 2 * HIGH)
+    inverse = inverse.transpose(2, 1, 3, 0)
+    col_fwd, col_inv = (
+        np.concatenate([table[:, :, lo:hi].reshape(-1, 2 * HIGH) for lo, hi in CHUNKS])
+        for table in (forward, inverse)
+    )
     step = np.arange(ROWS)
     angle = two_pi * ((step[:, None] * step[None, :]) % ROWS) / ROWS
     row_fwd = real_form(np.cos(angle), -np.sin(angle))
@@ -65,6 +69,7 @@
     return wide, narrow, col_twist, row_twist
 
 
+CHUNK_ROWS = [(2 * SLOTS * lo, 2 * SLOTS * (hi - lo)) for lo, hi in CHUNKS]
 COL_FWD = (0, 2 * BANDS)
 COL_INV = (2 * BANDS, 2 * BANDS)
 IN_FWD = (4 * BANDS, 2 * HIGH)
@@ -290,90 +295,96 @@
                 section[place, pl.ds(HIGH, HIGH)] = imag
 
     with jax.named_scope("column_128"):
-        forward = table(wide, COL_FWD)
-        for tile in range(TILES):
-            data = split(section[pl.ds(tile * FOLD * STRIP, FOLD * STRIP), :])
-            send_a[pl.ds(tile * 2 * BANDS, 2 * BANDS), :] = dot3(forward, data, ((1,), (1,)))
+        lanes = FOLD * STRIP
+        tiles = [split(section[pl.ds(tile * lanes, lanes), :]) for tile in range(TILES)]
+
+    rows_y = {step: lax.rem(place_y + step, 8) for step in (4, 3, 5, 2, 6, 1, 7, 0)}
+    rows_x = {step: 8 * lax.rem(place_x + step, 4) for step in (2, 1, 3, 0)}
+    rows_z = {1: 32 * (1 - place_z), 0: 32 * place_z}
+    peers = [rows_y[y] + (rows_x[x] + rows_z[z]) for y in rows_y for x in rows_x for z in rows_z if x or y or z]
 
     def exchange(source, target, send_sem, recv_sem):
-        def far_first(step, size):
-            return lax.rem(size // 2 + size + (1 - 2 * lax.rem(step, 2)) * ((step + 1) // 2), size)
-
-        def send_one(step, carry):
-            to_y = lax.rem(place_y + far_first(step // 8, 8), 8)
-            to_x = lax.rem(place_x + far_first(lax.rem(step // 2, 4), 4), 4)
-            to_z = lax.rem(place_z + 1 + lax.rem(step, 2), 2)
-            peer = to_z * 32 + to_x * 8 + to_y
+        msg = source.shape[0] // ROWS
+        here = pl.ds(me * msg, msg)
+        for peer in peers:
             pltpu.make_async_remote_copy(
-                src_ref=source.at[pl.ds(peer * MSG, MSG), :],
-                dst_ref=target.at[pl.ds(me * MSG, MSG), :],
+                src_ref=source.at[pl.ds(peer * msg, msg), :],
+                dst_ref=target.at[here, :],
                 send_sem=send_sem,
                 recv_sem=recv_sem,
                 device_id={"rows": peer},
                 device_id_type=MESH,
             ).start()
-            return carry
-
-        lax.fori_loop(0, ROWS - 1, send_one, 0)
-        target[pl.ds(me * MSG, MSG), :] = source[pl.ds(me * MSG, MSG), :]
-        every = pl.ds(0, (ROWS - 1) * MSG)
+        target[pl.ds(me * msg, msg), :] = source[pl.ds(me * msg, msg), :]
+        every = pl.ds(0, (ROWS - 1) * msg)
         return pltpu.make_async_remote_copy(
             src_ref=source.at[every, :],
             dst_ref=target.at[every, :],
             send_sem=send_sem,
             recv_sem=recv_sem,
-            device_id={"rows": lax.rem(me + 1, ROWS)},
+            device_id={"rows": peer_z},
             device_id_type=MESH,
         )
 
-    with jax.named_scope("exchange_a_start"):
-        first = exchange(send_a, recv_a, a_send, a_recv)
-    with jax.named_scope("exchange_a_wait"):
-        first.wait_recv()
-
-    with jax.named_scope("row_work"):
-        parts = [
-            jnp.concatenate(
-                [recv_a[pl.ds(sub, ROWS, stride=MSG), :], recv_a[pl.ds(SUB + sub, ROWS, stride=MSG), :]], axis=0
-            )
-            for sub in range(SUB)
-        ]
-        lanes = FOLD * STRIP
-        data = split(jnp.concatenate(parts, axis=1))
-        data = dot3(table(narrow, ROW_FWD), data, ((1,), (0,)))
-        twist_cos, twist_sin = row_twist[0], row_twist[1]
-        parts = []
-        for sub in range(SUB):
-            real, imag = data[:ROWS, sub * lanes : (sub + 1) * lanes], data[ROWS:, sub * lanes : (sub + 1) * lanes]
-            parts.append(jnp.concatenate(cmul((real, imag), (twist_cos, -twist_sin)), axis=1))
-        data = dot3(split(jnp.concatenate(parts, axis=0)), table(wide, IN_FWD), ((1,), (0,)))
-        parts = []
-        for sub in range(SUB):
-            rows = slice(sub * ROWS, (sub + 1) * ROWS)
-            real, imag = data[rows, :lanes], data[rows, lanes:]
-            parts.append(jnp.concatenate(cmul((real, imag), (pupil[0, sub], pupil[1, sub])), axis=1))
-        data = dot3(split(jnp.concatenate(parts, axis=0)), table(wide, IN_INV), ((1,), (0,)))
-        parts = []
-        for sub in range(SUB):
-            rows = slice(sub * ROWS, (sub + 1) * ROWS)
-            real, imag = data[rows, :lanes], data[rows, lanes:]
-            parts.append(jnp.concatenate(cmul((real, imag), (twist_cos, twist_sin)), axis=0))
-        data = dot3(table(narrow, ROW_INV), split(jnp.concatenate(parts, axis=1)), ((1,), (0,)))
-        for sub in range(SUB):
-            columns = slice(sub * lanes, (sub + 1) * lanes)
-            send_b[pl.ds(sub, ROWS, stride=MSG), :] = data[:ROWS, columns]
-            send_b[pl.ds(SUB + sub, ROWS, stride=MSG), :] = data[ROWS:, columns]
-
-    with jax.named_scope("exchange_b_start"):
-        second = exchange(send_b, recv_b, b_send, b_recv)
-    with jax.named_scope("exchange_b_wait"):
-        second.wait_recv()
-
-    with jax.named_scope("columns_back"):
-        inverse = table(wide, COL_INV)
-        for tile in range(TILES):
-            data = split(recv_b[pl.ds(tile * 2 * BANDS, 2 * BANDS), :].T)
-            section[pl.ds(tile * lanes, lanes), :] = dot3(data, inverse, ((1,), (0,)))
+    exchanges = []
+    for chunk, (start, size) in enumerate(CHUNK_ROWS):
+        with jax.named_scope("column_exchange"):
+            forward = table(wide, (COL_FWD[0] + start, size))
+            for tile in range(TILES):
+                send_a[chunk][pl.ds(tile * size, size), :] = dot3(forward, tiles[tile], ((1,), (1,)))
+            exchanges.append(exchange(send_a[chunk], recv_a[chunk], a_send.at[chunk], a_recv.at[chunk]))
+
+    twist_cos, twist_sin = row_twist[0], row_twist[1]
+    for chunk, (first, last) in enumerate(CHUNKS):
+        subs = last - first
+        msg = 2 * subs
+        with jax.named_scope("row_wait"):
+            exchanges[chunk].wait_recv()
+        with jax.named_scope("row_work"):
+            got = recv_a[chunk]
+            parts = [
+                jnp.concatenate([got[pl.ds(part * subs + sub, ROWS, stride=msg), :] for part in range(2)], axis=0)
+                for sub in range(subs)
+            ]
+            data = split(jnp.concatenate(parts, axis=1))
+            data = dot3(table(narrow, ROW_FWD), data, ((1,), (0,)))
+            parts = []
+            for sub in range(subs):
+                columns = slice(sub * lanes, (sub + 1) * lanes)
+                value = cmul((data[:ROWS, columns], data[ROWS:, columns]), (twist_cos, -twist_sin))
+                parts.append(jnp.concatenate(value, axis=1))
+            data = dot3(split(jnp.concatenate(parts, axis=0)), table(wide, IN_FWD), ((1,), (0,)))
+            parts = []
+            for sub in range(subs):
+                rows = slice(sub * ROWS, (sub + 1) * ROWS)
+                mask = (pupil[0, first + sub], pupil[1, first + sub])
+                parts.append(jnp.concatenate(cmul((data[rows, :lanes], data[rows, lanes:]), mask), axis=1))
+            data = dot3(split(jnp.concatenate(parts, axis=0)), table(wide, IN_INV), ((1,), (0,)))
+            parts = []
+            for sub in range(subs):
+                rows = slice(sub * ROWS, (sub + 1) * ROWS)
+                value = cmul((data[rows, :lanes], data[rows, lanes:]), (twist_cos, twist_sin))
+                parts.append(jnp.concatenate(value, axis=0))
+            data = dot3(table(narrow, ROW_INV), split(jnp.concatenate(parts, axis=1)), ((1,), (0,)))
+            for sub in range(subs):
+                columns = slice(sub * lanes, (sub + 1) * lanes)
+                for part in range(2):
+                    place = pl.ds(part * subs + sub, ROWS, stride=msg)
+                    send_b[chunk][place, :] = data[part * ROWS : (part + 1) * ROWS, columns]
+        with jax.named_scope("row_exchange"):
+            exchanges.append(exchange(send_b[chunk], recv_b[chunk], b_send.at[chunk], b_recv.at[chunk]))
+
+    for chunk, (start, size) in enumerate(CHUNK_ROWS):
+        with jax.named_scope("column_wait"):
+            exchanges[len(CHUNKS) + chunk].wait_recv()
+        with jax.named_scope("columns_back"):
+            inverse = table(wide, (COL_INV[0] + start, size))
+            for tile in range(TILES):
+                data = split(recv_b[chunk][pl.ds(tile * size, size), :].T)
+                value = dot3(data, inverse, ((1,), (0,)))
+                place = pl.ds(tile * lanes, lanes)
+                section[place, :] = value if chunk == 0 else section[place, :] + value
+    with jax.named_scope("columns_last"):
         for part in range(STRIP // 8):
             values = []
             for kap in range(LOW):
@@ -385,13 +396,14 @@
                 for plane in range(2):
                     out_ref[plane, pl.ds(8 * part, 8), pl.ds(HIGH * y1, HIGH)] = values[y1][plane]
 
-    first.wait_send()
-    second.wait_send()
+    for copy in exchanges:
+        copy.wait_send()
 
 
 def per_device(illum_tilts, index_layers, measured):
     wide, narrow, col_twist, row_twist = tables()
     vmem = pl.BlockSpec(memory_space=pltpu.VMEM)
+    messages = [pltpu.VMEM((2 * (hi - lo) * ROWS, FOLD * STRIP), jnp.float32) for lo, hi in CHUNKS]
     field = pl.pallas_call(
         kernel,
         out_shape=jax.ShapeDtypeStruct((2, STRIP, N), jnp.float32),
@@ -401,10 +413,10 @@
             pltpu.VMEM((GROUPS, STRIP, N // GROUPS), jnp.float32),
             pltpu.VMEM((2, LOW, STRIP, HIGH), jnp.float32),
             pltpu.VMEM((LOW * STRIP, 2 * HIGH), jnp.float32),
-            pltpu.VMEM((ROWS * MSG, FOLD * STRIP), jnp.float32),
-            pltpu.VMEM((ROWS * MSG, FOLD * STRIP), jnp.float32),
-            pltpu.VMEM((ROWS * MSG, FOLD * STRIP), jnp.float32),
-            pltpu.VMEM((ROWS * MSG, FOLD * STRIP), jnp.float32),
+            messages,
+            messages,
+            messages,
+            messages,
             pltpu.VMEM((2, SUB, ROWS, FOLD * STRIP), jnp.float32),
             pltpu.SMEM((1, 2), jnp.int32),
             pltpu.VMEM(wide.shape, jnp.bfloat16),
@@ -417,10 +429,10 @@
             pltpu.SemaphoreType.DMA((4,)),
             pltpu.SemaphoreType.REGULAR,
             pltpu.SemaphoreType.REGULAR,
-            pltpu.SemaphoreType.DMA,
-            pltpu.SemaphoreType.DMA,
-            pltpu.SemaphoreType.DMA,
-            pltpu.SemaphoreType.DMA,
+            pltpu.SemaphoreType.DMA((len(CHUNKS),)),
+            pltpu.SemaphoreType.DMA((len(CHUNKS),)),
+            pltpu.SemaphoreType.DMA((len(CHUNKS),)),
+            pltpu.SemaphoreType.DMA((len(CHUNKS),)),
             pltpu.SemaphoreType.DMA((6,)),
         ],
         compiler_params=pltpu.CompilerParams(

time: 48.1 us -> 44.9 us (0.933)
  Pallas kernels: 46.1 us -> 42.8 us
    pallas_call x1, Pallas kernels: 46.1 us -> 42.8 us  [per_device(): pl.pallas_call(kernel, out_shape=jax.ShapeDtypeStruct((2, STRIP, N), jnp....]
where the time goes in v3:
time: 44.9 us; the launch traced here: 44.7 us
  Pallas kernels  42.8 us (95%)
  other arithmetic  1.89 us (4%)
    pallas_call x1, Pallas kernels, per_device(): pl.pallas_call(kernel, out_shape=jax.ShapeDtypeStruct((2, STRIP, N), jnp....  42.8 us
    sub x1, other arithmetic, per_device(): return field[None] - measured  1.89 us

profile of v3, /device:TPU:1, one launch (start us, length us, event | category | flops | bytes accessed | tf_op | source)
XLA Modules:
  0.0 44.7 jit_solution(10483785598955181708)
XLA Ops:
  0.0 0.0 copy-start
  0.0 42.8 %shard_map.73 = f32[2,32,2048]{2,1,0:T(8,128)} custom-call(s32[1,2]{1,0:T(1,128)} %tilts_hbm.1, f32[32,256]{1,0:T(8,128)} %bitcast.3, bf16[2,832,256]{2,1,0:T(8,128)(2,1)} %constant.8.clone.wide_hbm, bf16[2,256,128]{2,1,0:T(8,128)(2,1)} %constant.9.clone.narrow_hbm, f32[2,16,128]{2,1,0:T(8,128)} %constant.10.clone.col_hbm, f32[2,64,128]{2,1,0:T(8,128)} %constant.11.clone.row_hbm), custom_call_target="tpu_custom_call" | custom-call | tf_op jit(solution)/shard_map/pallas_call | solution.py:407
  42.8 0.0 copy-done
  42.8 1.9 %bitcast_subtract_fusion = f32[1,2,32,2048]{3,2,1,0:T(8,128)} fusion(f32[1,2,32,2048]{3,2,1,0:T(8,128)S(1)} %copy-done, f32[2,32,2048]{2,1,0:T(8,128)} %shard_map.73), kind=kLoop, calls=%fused_computation | loop fusion | flops 131072 | bytes 1572864 | tf_op jit(solution)/shard_map/sub | solution.py:449
Async XLA Ops:
  0.0 42.8 %copy-start = (f32[1,2,32,2048]{3,2,1,0:T(8,128)S(1)}, f32[1,2,32,2048]{3,2,1,0:T(8,128)}, u32[]{:S(2)}) copy-start(f32[1,2,32,2048]{3,2,1,0:T(8,128)} %param.9) | copy-start | bytes 1572868

commit v4 on v3

--- a/solution.py
+++ b/solution.py
@@ -21,7 +21,7 @@
 BANDS = 80
 SUB = 5
 FOLD = 4
-CHUNKS = ((0, 2), (2, 4), (4, 5))
+CHUNKS = ((0, 1), (1, 2), (2, 3), (3, 5))
 TILES = LOW // FOLD
 SLOTS = BANDS // SUB
 
@@ -174,7 +174,7 @@
     tilts_hbm, index_ref, wide_hbm, narrow_hbm, col_hbm, row_hbm, out_ref,
     strip, incident, section, send_a, recv_a, send_b, recv_b, pupil,
     tilts, wide, narrow, col_twist, row_twist,
-    gather_send, gather_recv, pass_send, pass_recv, plane_sem, pair_sem, a_send, a_recv, b_send, b_recv, load_sems,
+    gather_send, gather_recv, pass_send, pass_recv, line_sem, plane_sem, pair_sem, a_send, a_recv, b_send, b_recv, load_sems,
 ):
     group = lax.axis_index("group")
     me = lax.axis_index("rows")
@@ -198,29 +198,32 @@
         rows = pl.ds(place[0], place[1])
         return ref[0, rows, :], ref[1, rows, :]
 
-    side = lax.rem(group, 2)
-    partner = group + 1 - 2 * side
+    partner = group + 1 - 2 * lax.rem(group, 2)
+    group_next, group_last = lax.rem(group + 2, GROUPS), lax.rem(group + 6, GROUPS)
+    group_far = lax.rem(group + 4, GROUPS)
+    other_next, other_last, other_far = (lax.rem(partner + step, GROUPS) for step in (2, 6, 4))
     place_z, place_x, place_y = me // 32, lax.rem(me // 8, 4), lax.rem(me, 8)
-    peers_y = [me - place_y + lax.rem(place_y + step, 8) for step in range(1, 8)]
-    peers_x = [me + 8 * (lax.rem(place_x + step, 4) - place_x) for step in range(1, 4)]
+    peers_y = [me - place_y + lax.rem(place_y + step, 8) for step in (2, 6, 1, 7)]
+    peers_x = [me + 8 * (lax.rem(place_x + step, 4) - place_x) for step in (2, 1, 3)]
     peer_z = me + 32 * (1 - 2 * place_z)
-    peers_group = [lax.rem(group + 2 * step, GROUPS) for step in (2, 1, 3)]
 
     def signal(sem, axis, peer):
         pl.semaphore_signal(sem, inc=1, device_id={axis: peer}, device_id_type=MESH)
 
     with jax.named_scope("greet"):
         barrier = pltpu.get_barrier_semaphore()
-        for peer in peers_group + [partner]:
+        for peer in (group_next, group_last, partner, other_next, other_last):
             signal(barrier, "group", peer)
         for peer in peers_y + peers_x + [peer_z]:
             signal(barrier, "rows", peer)
-        pl.semaphore_wait(barrier, 15)
-
-    def piece(owner, sems, slot, peer):
+        pl.semaphore_wait(barrier, 13)
+
+    half = STRIP // 2
+
+    def piece(owner, rows, sems, slot, peer, own=False):
         return pltpu.make_async_remote_copy(
-            src_ref=strip.at[owner],
-            dst_ref=strip.at[owner],
+            src_ref=index_ref.at[rows, :] if own else strip.at[owner, rows, :],
+            dst_ref=strip.at[owner, rows, :],
             send_sem=sems[0].at[slot],
             recv_sem=sems[1].at[slot],
             device_id={"group": peer},
@@ -228,18 +231,22 @@
         )
 
     gather_sems, pass_sems = (gather_send, gather_recv), (pass_send, pass_recv)
+    whole, top, bottom = pl.ds(0, STRIP), pl.ds(0, half), pl.ds(half, half)
+    copies = []
+
+    def send(*args, own=False):
+        copies.append(piece(*args, own=own))
+        copies[-1].start()
+
+    def receive(*args):
+        piece(*args).wait_recv()
+
     with jax.named_scope("gather_start"):
-        loads[1].wait()
-        gathers = [piece(group, gather_sems, slot, peer) for slot, peer in enumerate(peers_group)]
-        passes = [piece(group, pass_sems, 3, partner)]
-        for copy in gathers + passes:
-            copy.start()
-    with jax.named_scope("report"):
-        for peer in peers_x:
-            signal(plane_sem, "rows", peer)
-        pl.semaphore_wait(plane_sem, 3)
-        signal(pair_sem, "rows", peer_z)
-        pl.semaphore_wait(pair_sem, 1)
+        send(group, whole, gather_sems, 0, group_next, own=True)
+        send(group, whole, gather_sems, 1, group_last, own=True)
+        send(group, whole, pass_sems, 0, partner, own=True)
+        for peer in peers_y[:2]:
+            signal(line_sem, "rows", peer)
 
     with jax.named_scope("incident_pupil"):
         loads[0].wait()
@@ -265,16 +272,27 @@
             pupil[1, sub] = imag
 
     with jax.named_scope("gather_wait"):
-        for slot, step in ((1, 3), (2, 1), (0, 2)):
-            gathers[slot].wait_recv()
-            copy = piece(lax.rem(group + 2 * step, GROUPS), pass_sems, slot, partner)
-            copy.start()
-            passes.append(copy)
-        for copy in passes:
-            copy.wait()
-        for copy in gathers:
-            copy.wait_send()
-        for place in (2, 3, 4, 5):
+        receive(group_last, whole, gather_sems, 0, group_next)
+        send(group_last, top, gather_sems, 2, group_next)
+        send(group_last, top, pass_sems, 3, other_next)
+        send(group_last, whole, pass_sems, 1, partner)
+        receive(group_next, whole, gather_sems, 1, group_last)
+        send(group_next, bottom, gather_sems, 3, group_last)
+        send(group_next, bottom, pass_sems, 4, other_last)
+        send(group_next, whole, pass_sems, 2, partner)
+        pl.semaphore_wait(line_sem, 2)
+        for peer in peers_x:
+            signal(plane_sem, "rows", peer)
+        pl.semaphore_wait(plane_sem, 3)
+        signal(pair_sem, "rows", peer_z)
+        receive(group_far, top, gather_sems, 2, group_next)
+        receive(group_far, bottom, gather_sems, 3, group_last)
+        pl.semaphore_wait(pair_sem, 1)
+        for slot, (owner, rows) in enumerate(
+            [(group, whole), (group_last, whole), (group_next, whole), (group_far, top), (group_far, bottom)]
+        ):
+            receive(owner, rows, pass_sems, slot, partner)
+        for place in (1, 2, 3, 4, 5):
             loads[place].wait()
 
     with jax.named_scope("screen_dft16"):
@@ -298,7 +316,10 @@
         lanes = FOLD * STRIP
         tiles = [split(section[pl.ds(tile * lanes, lanes), :]) for tile in range(TILES)]
 
-    rows_y = {step: lax.rem(place_y + step, 8) for step in (4, 3, 5, 2, 6, 1, 7, 0)}
+    side = lax.rem(group, 2)
+    rows_y = {
+        step: lax.rem(place_y + (1 - side) * step + side * (8 - step), 8) for step in (4, 3, 5, 2, 6, 1, 7, 0)
+    }
     rows_x = {step: 8 * lax.rem(place_x + step, 4) for step in (2, 1, 3, 0)}
     rows_z = {1: 32 * (1 - place_z), 0: 32 * place_z}
     peers = [rows_y[y] + (rows_x[x] + rows_z[z]) for y in rows_y for x in rows_x for z in rows_z if x or y or z]
@@ -396,7 +417,7 @@
                 for plane in range(2):
                     out_ref[plane, pl.ds(8 * part, 8), pl.ds(HIGH * y1, HIGH)] = values[y1][plane]
 
-    for copy in exchanges:
+    for copy in copies + exchanges:
         copy.wait_send()
 
 
@@ -423,10 +444,11 @@
             pltpu.VMEM(narrow.shape, jnp.bfloat16),
             pltpu.VMEM(col_twist.shape, jnp.float32),
             pltpu.VMEM(row_twist.shape, jnp.float32),
-            pltpu.SemaphoreType.DMA((3,)),
-            pltpu.SemaphoreType.DMA((3,)),
             pltpu.SemaphoreType.DMA((4,)),
             pltpu.SemaphoreType.DMA((4,)),
+            pltpu.SemaphoreType.DMA((5,)),
+            pltpu.SemaphoreType.DMA((5,)),
+            pltpu.SemaphoreType.REGULAR,
             pltpu.SemaphoreType.REGULAR,
             pltpu.SemaphoreType.REGULAR,
             pltpu.SemaphoreType.DMA((len(CHUNKS),)),

time: 44.9 us -> 44 us (0.980)
  Pallas kernels: 42.8 us -> 42 us
    pallas_call x1, Pallas kernels: 42.8 us -> 42 us  [per_device(): pl.pallas_call(kernel, out_shape=jax.ShapeDtypeStruct((2, STRIP, N), jnp....]
where the time goes in v4:
time: 44 us; the launch traced here: 43.9 us
  Pallas kernels  42 us (95%)
  other arithmetic  1.89 us (4%)
    pallas_call x1, Pallas kernels, per_device(): pl.pallas_call(kernel, out_shape=jax.ShapeDtypeStruct((2, STRIP, N), jnp....  42 us
    sub x1, other arithmetic, per_device(): return field[None] - measured  1.89 us

profile of v4, /device:TPU:1, one launch (start us, length us, event | category | flops | bytes accessed | tf_op | source)
XLA Modules:
  0.0 43.9 jit_solution(11816554065147518956)
XLA Ops:
  0.0 0.0 copy-start
  0.0 42.0 %shard_map.73 = f32[2,32,2048]{2,1,0:T(8,128)} custom-call(s32[1,2]{1,0:T(1,128)} %tilts_hbm.1, f32[32,256]{1,0:T(8,128)} %bitcast.3, bf16[2,832,256]{2,1,0:T(8,128)(2,1)} %constant.8.clone.wide_hbm, bf16[2,256,128]{2,1,0:T(8,128)(2,1)} %constant.9.clone.narrow_hbm, f32[2,16,128]{2,1,0:T(8,128)} %constant.10.clone.col_hbm, f32[2,64,128]{2,1,0:T(8,128)} %constant.11.clone.row_hbm), custom_call_target="tpu_custom_call" | custom-call | tf_op jit(solution)/shard_map/pallas_call | solution.py:428
  42.0 0.0 copy-done
  42.0 1.9 %bitcast_subtract_fusion = f32[1,2,32,2048]{3,2,1,0:T(8,128)} fusion(f32[1,2,32,2048]{3,2,1,0:T(8,128)S(1)} %copy-done, f32[2,32,2048]{2,1,0:T(8,128)} %shard_map.73), kind=kLoop, calls=%fused_computation | loop fusion | flops 131072 | bytes 1572864 | tf_op jit(solution)/shard_map/sub | solution.py:471
Async XLA Ops:
  0.0 42.0 %copy-start = (f32[1,2,32,2048]{3,2,1,0:T(8,128)S(1)}, f32[1,2,32,2048]{3,2,1,0:T(8,128)}, u32[]{:S(2)}) copy-start(f32[1,2,32,2048]{3,2,1,0:T(8,128)} %param.9) | copy-start | bytes 1572868

commit v5 on v4

--- a/solution.py
+++ b/solution.py
@@ -157,7 +157,9 @@
     def one(x, y):
         return lax.dot_general(x, y, (dims, ((), ())), preferred_element_type=jnp.float32)
 
-    return one(a[0], b[0]) + (one(a[0], b[1]) + one(a[1], b[0]))
+    rows = a[0].shape[0]
+    both = one(jnp.concatenate(a, axis=0), b[0])
+    return both[:rows] + (both[rows:] + one(a[0], b[1]))
 
 
 def pupil_parts(freq_rows, freq_cols):
@@ -178,21 +180,6 @@
 ):
     group = lax.axis_index("group")
     me = lax.axis_index("rows")
-    loads = [
-        pltpu.make_async_copy(source, target, load_sems.at[place])
-        for place, (source, target) in enumerate(
-            [
-                (tilts_hbm, tilts),
-                (index_ref, strip.at[group]),
-                (col_hbm, col_twist),
-                (wide_hbm, wide),
-                (narrow_hbm, narrow),
-                (row_hbm, row_twist),
-            ]
-        )
-    ]
-    for load in loads:
-        load.start()
 
     def table(ref, place):
         rows = pl.ds(place[0], place[1])
@@ -216,13 +203,28 @@
             signal(barrier, "group", peer)
         for peer in peers_y + peers_x + [peer_z]:
             signal(barrier, "rows", peer)
+        loads = [
+            pltpu.make_async_copy(source, target, load_sems.at[place])
+            for place, (source, target) in enumerate(
+                [
+                    (tilts_hbm, tilts),
+                    (index_ref, strip.at[group]),
+                    (col_hbm, col_twist),
+                    (wide_hbm, wide),
+                    (narrow_hbm, narrow),
+                    (row_hbm, row_twist),
+                ]
+            )
+        ]
+        for load in loads:
+            load.start()
         pl.semaphore_wait(barrier, 13)
 
     half = STRIP // 2
 
-    def piece(owner, rows, sems, slot, peer, own=False):
+    def piece(owner, rows, sems, slot, peer):
         return pltpu.make_async_remote_copy(
-            src_ref=index_ref.at[rows, :] if own else strip.at[owner, rows, :],
+            src_ref=strip.at[owner, rows, :],
             dst_ref=strip.at[owner, rows, :],
             send_sem=sems[0].at[slot],
             recv_sem=sems[1].at[slot],
@@ -234,17 +236,27 @@
     whole, top, bottom = pl.ds(0, STRIP), pl.ds(0, half), pl.ds(half, half)
     copies = []
 
-    def send(*args, own=False):
-        copies.append(piece(*args, own=own))
+    def send(*args):
+        copies.append(piece(*args))
         copies[-1].start()
 
     def receive(*args):
         piece(*args).wait_recv()
 
+    def screen(owner, rows=whole):
+        for side_half in range(2):
+            contrast = strip[owner, rows, pl.ds(HIGH * side_half, HIGH)]
+            y1 = 2 * owner + side_half
+            value = (incident[0, y1, rows, :], incident[1, y1, rows, :])
+            value = cmul(sincos_small(contrast * (2.0 * math.pi * THICKNESS)), value)
+            incident[0, y1, rows, :] = value[0]
+            incident[1, y1, rows, :] = value[1]
+
     with jax.named_scope("gather_start"):
-        send(group, whole, gather_sems, 0, group_next, own=True)
-        send(group, whole, gather_sems, 1, group_last, own=True)
-        send(group, whole, pass_sems, 0, partner, own=True)
+        loads[1].wait()
+        send(group, whole, gather_sems, 0, group_next)
+        send(group, whole, gather_sems, 1, group_last)
+        send(group, whole, pass_sems, 0, partner)
         for peer in peers_y[:2]:
             signal(line_sem, "rows", peer)
 
@@ -272,6 +284,9 @@
             pupil[1, sub] = imag
 
     with jax.named_scope("gather_wait"):
+        pl.semaphore_wait(line_sem, 2)
+        for peer in peers_x:
+            signal(plane_sem, "rows", peer)
         receive(group_last, whole, gather_sems, 0, group_next)
         send(group_last, top, gather_sems, 2, group_next)
         send(group_last, top, pass_sems, 3, other_next)
@@ -280,19 +295,22 @@
         send(group_next, bottom, gather_sems, 3, group_last)
         send(group_next, bottom, pass_sems, 4, other_last)
         send(group_next, whole, pass_sems, 2, partner)
-        pl.semaphore_wait(line_sem, 2)
-        for peer in peers_x:
-            signal(plane_sem, "rows", peer)
         pl.semaphore_wait(plane_sem, 3)
         signal(pair_sem, "rows", peer_z)
+        for owner in (group, group_last, group_next):
+            screen(owner)
+        receive(partner, whole, pass_sems, 0, partner)
+        screen(partner)
         receive(group_far, top, gather_sems, 2, group_next)
         receive(group_far, bottom, gather_sems, 3, group_last)
-        pl.semaphore_wait(pair_sem, 1)
-        for slot, (owner, rows) in enumerate(
-            [(group, whole), (group_last, whole), (group_next, whole), (group_far, top), (group_far, bottom)]
-        ):
-            receive(owner, rows, pass_sems, slot, partner)
-        for place in (1, 2, 3, 4, 5):
+        screen(group_far)
+        for slot, (owner, rows) in enumerate([(other_last, whole), (other_next, whole)]):
+            receive(owner, rows, pass_sems, 1 + slot, partner)
+            screen(owner)
+        for slot, rows in enumerate((top, bottom)):
+            receive(other_far, rows, pass_sems, 3 + slot, partner)
+        screen(other_far)
+        for place in (2, 3, 4, 5):
             loads[place].wait()
 
     with jax.named_scope("screen_dft16"):
@@ -300,10 +318,7 @@
             rows = pl.ds(8 * part, 8)
             values = []
             for y1 in range(LOW):
-                lanes = pl.ds(HIGH * (y1 % 2), HIGH)
-                contrast = strip[y1 // 2, rows, lanes]
-                screen = sincos_small(contrast * (2.0 * math.pi * THICKNESS))
-                values.append(cmul(screen, (incident[0, y1, rows, :], incident[1, y1, rows, :])))
+                values.append((incident[0, y1, rows, :], incident[1, y1, rows, :]))
             values = dft16(values, -1)
             for kap in range(LOW):
                 twist = (col_twist[0, pl.ds(kap, 1), :], -col_twist[1, pl.ds(kap, 1), :])
@@ -347,6 +362,7 @@
             device_id_type=MESH,
         )
 
+    pl.semaphore_wait(pair_sem, 1)
     exchanges = []
     for chunk, (start, size) in enumerate(CHUNK_ROWS):
         with jax.named_scope("column_exchange"):

time: 44 us -> 43.2 us (0.982)
  Pallas kernels: 42 us -> 40.8 us
    pallas_call x1, Pallas kernels: 42 us -> 40.8 us  [per_device(): pl.pallas_call(kernel, out_shape=jax.ShapeDtypeStruct((2, STRIP, N), jnp....]
where the time goes in v5:
time: 43.2 us; the launch traced here: 42.7 us
  Pallas kernels  40.8 us (94%)
  other arithmetic  1.89 us (4%)
    pallas_call x1, Pallas kernels, per_device(): pl.pallas_call(kernel, out_shape=jax.ShapeDtypeStruct((2, STRIP, N), jnp....  40.8 us
    sub x1, other arithmetic, per_device(): return field[None] - measured  1.89 us

profile of v5, /device:TPU:1, one launch (start us, length us, event | category | flops | bytes accessed | tf_op | source)
XLA Modules:
  0.0 42.7 jit_solution(13053514302868164893)
XLA Ops:
  0.0 0.0 copy-start
  0.0 40.8 %shard_map.73 = f32[2,32,2048]{2,1,0:T(8,128)} custom-call(s32[1,2]{1,0:T(1,128)} %tilts_hbm.1, f32[32,256]{1,0:T(8,128)} %bitcast.3, bf16[2,832,256]{2,1,0:T(8,128)(2,1)} %constant.8.clone.wide_hbm, bf16[2,256,128]{2,1,0:T(8,128)(2,1)} %constant.9.clone.narrow_hbm, f32[2,16,128]{2,1,0:T(8,128)} %constant.10.clone.col_hbm, f32[2,64,128]{2,1,0:T(8,128)} %constant.11.clone.row_hbm), custom_call_target="tpu_custom_call" | custom-call | tf_op jit(solution)/shard_map/pallas_call | solution.py:444
  40.8 0.0 copy-done
  40.8 1.9 %bitcast_subtract_fusion = f32[1,2,32,2048]{3,2,1,0:T(8,128)} fusion(f32[1,2,32,2048]{3,2,1,0:T(8,128)S(1)} %copy-done, f32[2,32,2048]{2,1,0:T(8,128)} %shard_map.73), kind=kLoop, calls=%fused_computation | loop fusion | flops 131072 | bytes 1572864 | tf_op jit(solution)/shard_map/sub | solution.py:487
Async XLA Ops:
  0.0 40.8 %copy-start = (f32[1,2,32,2048]{3,2,1,0:T(8,128)S(1)}, f32[1,2,32,2048]{3,2,1,0:T(8,128)}, u32[]{:S(2)}) copy-start(f32[1,2,32,2048]{3,2,1,0:T(8,128)} %param.9) | copy-start | bytes 1572868

commit v6 on v5

--- a/solution.py
+++ b/solution.py
@@ -173,9 +173,9 @@
 
 
 def kernel(
-    tilts_hbm, index_ref, wide_hbm, narrow_hbm, col_hbm, row_hbm, out_ref,
+    tilts_hbm, index_ref, wide_hbm, narrow_hbm, col_hbm, row_hbm, out_hbm,
     strip, incident, section, send_a, recv_a, send_b, recv_b, pupil,
-    tilts, wide, narrow, col_twist, row_twist,
+    tilts, wide, narrow, col_twist, row_twist, out_ref, out_sems,
     gather_send, gather_recv, pass_send, pass_recv, line_sem, plane_sem, pair_sem, a_send, a_recv, b_send, b_recv, load_sems,
 ):
     group = lax.axis_index("group")
@@ -421,6 +421,7 @@
                 value = dot3(data, inverse, ((1,), (0,)))
                 place = pl.ds(tile * lanes, lanes)
                 section[place, :] = value if chunk == 0 else section[place, :] + value
+    results = []
     with jax.named_scope("columns_last"):
         for part in range(STRIP // 8):
             values = []
@@ -432,20 +433,24 @@
             for y1 in range(LOW):
                 for plane in range(2):
                     out_ref[plane, pl.ds(8 * part, 8), pl.ds(HIGH * y1, HIGH)] = values[y1][plane]
+            rows = pl.ds(8 * part, 8)
+            results.append(pltpu.make_async_copy(out_ref.at[:, rows, :], out_hbm.at[:, rows, :], out_sems.at[part]))
+            results[-1].start()
 
     for copy in copies + exchanges:
         copy.wait_send()
+    for copy in results:
+        copy.wait()
 
 
 def per_device(illum_tilts, index_layers, measured):
     wide, narrow, col_twist, row_twist = tables()
-    vmem = pl.BlockSpec(memory_space=pltpu.VMEM)
     messages = [pltpu.VMEM((2 * (hi - lo) * ROWS, FOLD * STRIP), jnp.float32) for lo, hi in CHUNKS]
     field = pl.pallas_call(
         kernel,
         out_shape=jax.ShapeDtypeStruct((2, STRIP, N), jnp.float32),
         in_specs=[pl.BlockSpec(memory_space=pltpu.HBM)] * 6,
-        out_specs=vmem,
+        out_specs=pl.BlockSpec(memory_space=pltpu.HBM),
         scratch_shapes=[
             pltpu.VMEM((GROUPS, STRIP, N // GROUPS), jnp.float32),
             pltpu.VMEM((2, LOW, STRIP, HIGH), jnp.float32),
@@ -460,6 +465,8 @@
             pltpu.VMEM(narrow.shape, jnp.bfloat16),
             pltpu.VMEM(col_twist.shape, jnp.float32),
             pltpu.VMEM(row_twist.shape, jnp.float32),
+            pltpu.VMEM((2, STRIP, N), jnp.float32),
+            pltpu.SemaphoreType.DMA((STRIP // 8,)),
             pltpu.SemaphoreType.DMA((4,)),
             pltpu.SemaphoreType.DMA((4,)),
             pltpu.SemaphoreType.DMA((5,)),

time: 43.2 us -> 43.1 us (level)
  no operation moved by 1% of the time
where the time goes in v6:
time: 43.1 us; the launch traced here: 42.7 us
  Pallas kernels  40.8 us (95%)
  other arithmetic  1.89 us (4%)
    pallas_call x1, Pallas kernels, per_device(): pl.pallas_call(kernel, out_shape=jax.ShapeDtypeStruct((2, STRIP, N), jnp....  40.8 us
    sub x1, other arithmetic, per_device(): return field[None] - measured  1.89 us

profile of v6, /device:TPU:1, one launch (start us, length us, event | category | flops | bytes accessed | tf_op | source)
XLA Modules:
  0.0 42.7 jit_solution(642523574476655353)
XLA Ops:
  0.0 0.0 copy-start
  0.0 40.8 %shard_map.73 = f32[2,32,2048]{2,1,0:T(8,128)} custom-call(s32[1,2]{1,0:T(1,128)} %tilts_hbm.1, f32[32,256]{1,0:T(8,128)} %bitcast.3, bf16[2,832,256]{2,1,0:T(8,128)(2,1)} %constant.8.clone.wide_hbm, bf16[2,256,128]{2,1,0:T(8,128)(2,1)} %constant.9.clone.narrow_hbm, f32[2,16,128]{2,1,0:T(8,128)} %constant.10.clone.col_hbm, f32[2,64,128]{2,1,0:T(8,128)} %constant.11.clone.row_hbm), custom_call_target="tpu_custom_call" | custom-call | tf_op jit(solution)/shard_map/pallas_call | solution.py:449
  40.8 0.0 copy-done
  40.8 1.9 %bitcast_subtract_fusion = f32[1,2,32,2048]{3,2,1,0:T(8,128)} fusion(f32[1,2,32,2048]{3,2,1,0:T(8,128)S(1)} %copy-done, f32[2,32,2048]{2,1,0:T(8,128)} %shard_map.73), kind=kLoop, calls=%fused_computation | loop fusion | flops 131072 | bytes 1572864 | tf_op jit(solution)/shard_map/sub | solution.py:494
Async XLA Ops:
  0.0 40.8 %copy-start = (f32[1,2,32,2048]{3,2,1,0:T(8,128)S(1)}, f32[1,2,32,2048]{3,2,1,0:T(8,128)}, u32[]{:S(2)}) copy-start(f32[1,2,32,2048]{3,2,1,0:T(8,128)} %param.9) | copy-start | bytes 1572868

commit v7 on v6

--- a/solution.py
+++ b/solution.py
@@ -21,7 +21,7 @@
 BANDS = 80
 SUB = 5
 FOLD = 4
-CHUNKS = ((0, 1), (1, 2), (2, 3), (3, 5))
+CHUNKS = ((0, 1), (1, 3), (3, 5))
 TILES = LOW // FOLD
 SLOTS = BANDS // SUB
 

time: 43.1 us -> 43.1 us (level)
  no operation moved by 1% of the time
where the time goes in v7:
time: 43.1 us; the launch traced here: 42.8 us
  Pallas kernels  40.8 us (95%)
  other arithmetic  1.89 us (4%)
    pallas_call x1, Pallas kernels, per_device(): pl.pallas_call(kernel, out_shape=jax.ShapeDtypeStruct((2, STRIP, N), jnp....  40.8 us
    sub x1, other arithmetic, per_device(): return field[None] - measured  1.89 us

profile of v7, /device:TPU:1, one launch (start us, length us, event | category | flops | bytes accessed | tf_op | source)
XLA Modules:
  0.0 42.8 jit_solution(12969798040701755143)
XLA Ops:
  0.0 0.0 copy-start
  0.0 40.8 %shard_map.73 = f32[2,32,2048]{2,1,0:T(8,128)} custom-call(s32[1,2]{1,0:T(1,128)} %tilts_hbm.1, f32[32,256]{1,0:T(8,128)} %bitcast.3, bf16[2,832,256]{2,1,0:T(8,128)(2,1)} %constant.8.clone.wide_hbm, bf16[2,256,128]{2,1,0:T(8,128)(2,1)} %constant.9.clone.narrow_hbm, f32[2,16,128]{2,1,0:T(8,128)} %constant.10.clone.col_hbm, f32[2,64,128]{2,1,0:T(8,128)} %constant.11.clone.row_hbm), custom_call_target="tpu_custom_call" | custom-call | tf_op jit(solution)/shard_map/pallas_call | solution.py:449
  40.9 0.0 copy-done
  40.9 1.9 %bitcast_subtract_fusion = f32[1,2,32,2048]{3,2,1,0:T(8,128)} fusion(f32[1,2,32,2048]{3,2,1,0:T(8,128)S(1)} %copy-done, f32[2,32,2048]{2,1,0:T(8,128)} %shard_map.73), kind=kLoop, calls=%fused_computation | loop fusion | flops 131072 | bytes 1572864 | tf_op jit(solution)/shard_map/sub | solution.py:494
Async XLA Ops:
  0.0 40.9 %copy-start = (f32[1,2,32,2048]{3,2,1,0:T(8,128)S(1)}, f32[1,2,32,2048]{3,2,1,0:T(8,128)}, u32[]{:S(2)}) copy-start(f32[1,2,32,2048]{3,2,1,0:T(8,128)} %param.9) | copy-start | bytes 1572868
